TPU v7x, 128 devices: a whole 4x4x4 slice. The times are simulated.
128 devices in a mesh: dp: 16 (over z, x), tensor: 8 (over y, core).
Axes of the slice: x: 4, y: 4, z: 4, core: 2. Of those that a mesh axis runs over, the one named last changes fastest.
Arguments:
- activations: bfloat16 [4096, 3072], P('dp', 'tensor'), may hold values from -6 to 6
- act_grad: bfloat16 [4096, 12288], P('dp', 'tensor'), may hold values from -6 to 6
- up_weight: bfloat16 [3072, 12288], P('dp', 'tensor'), may hold values from -0.15625 to 0.15625
- width_steps: int32 [4096], P('dp'), may hold values from 1 to 8
Outputs:
- input_grad: bfloat16 [4096, 3072], P('dp', 'tensor')
- weight_grad: bfloat16 [3072, 12288], P('dp', 'tensor')
Inputs may be any that keep to these rules, and one draw needn't show every extreme that they name: Token r uses the hidden units below 1536 * width_steps[r].
All inputs are finite; a program needn't handle non-finite values.
Results may differ from a plain program's by a relative error of at most 0.022.
Values may be sent and summed in bfloat16 or wider, within the bound.
A program may use at most 128 MiB of HBM per device.

v0:
```python
import math

import jax
import jax.numpy as jnp
from jax import lax
from jax.sharding import PartitionSpec as P

FF = 12288


def shards(activations, act_grad, up_weight, width_steps):
    my_index = lax.axis_index("tensor")
    columns = up_weight.shape[1]
    half_cols = columns // 2
    block_cols = FF // 8
    tok_rows = activations.shape[0]
    whole_x = lax.all_gather(activations, "tensor", axis=1, tiled=True)
    own_start = my_index * columns
    second_start = own_start + half_cols
    weights = lax.all_gather(up_weight, "dp", axis=0, tiled=True)
    first_block = own_start // block_cols
    second_block = second_start // block_cols
    column_block = jnp.where(jnp.arange(columns) < half_cols, first_block, second_block)
    grad_scale = 1.0 / math.sqrt(tok_rows * lax.axis_size("dp"))
    preact = jnp.dot(whole_x, weights, preferred_element_type=jnp.float32)
    in_use = column_block[None, :] < width_steps[:, None]
    slope = jnp.where(in_use, 2.0 * jnp.maximum(preact, 0.0), 0.0)
    hidden_grad = (act_grad.astype(jnp.float32) * slope).astype(jnp.bfloat16)
    partial_x = jnp.dot(hidden_grad, weights.T, preferred_element_type=jnp.float32)
    product = lax.dot_general(
        whole_x, hidden_grad, (((0,), (0,)), ((), ())), preferred_element_type=jnp.float32
    )
    grad_rows = lax.psum_scatter(
        (product * grad_scale).astype(jnp.bfloat16), "dp", scatter_dimension=0, tiled=True
    )
    input_grad = lax.psum_scatter(
        partial_x.astype(jnp.bfloat16), "tensor", scatter_dimension=1, tiled=True
    )
    return (input_grad, grad_rows)


def solution(mesh):
    placed = (P("dp", "tensor"), P("dp", "tensor"), P("dp", "tensor"), P("dp"))
    return jax.shard_map(
        shards,
        mesh=mesh,
        in_specs=placed,
        out_specs=(P("dp", "tensor"), P("dp", "tensor")),
        check_vma=False,
    )
```

profile of v0, /device:TPU:1, one launch (start us, length us, event | category | flops | bytes accessed | tf_op | source)
XLA Modules:
  0.0 255.2 jit_solution(12469248334051356824)
XLA Ops:
  7.2 0.0 all-gather.3.cloned.1.call-start
  7.2 0.7 all-gather.3.cloned.1.call-update
  7.9 0.0 all-gather.5.cloned.1.call-start
  7.9 0.7 all-gather.5.cloned.1.call-update
  8.6 0.0 reduce-scatter.7.cloned.1.call-start
  8.7 29.3 %all-gather.3.cloned.1.call-done = bf16[256,3072]{1,0:T(8,128)(2,1)} async-done(((bf16[256,384]{1,0:T(8,128)(2,1)}), bf16[256,3072]{1,0:T(8,128)(2,1)}) %all-gather.3.cloned.1.call-update) | async-done | bytes 1572880 | tf_op jit(solution)/shard_map/all_gather | solution.py:17
  38.0 77.6 %all-gather.5.cloned.1.call-done = bf16[3072,1536]{1,0:T(8,128)(2,1)} async-done(((bf16[192,1536]{1,0:T(8,128)(2,1)}), bf16[3072,1536]{1,0:T(8,128)(2,1)}) %all-gather.5.cloned.1.call-update) | async-done | bytes 9437200 | tf_op jit(solution)/shard_map/all_gather | solution.py:20
  115.6 0.0 copy-start
  115.6 7.1 %fusion.4 = bf16[256,1536]{1,0:T(8,128)(2,1)S(1)} fusion(bf16[256,3072]{1,0:T(8,128)(2,1)} %all-gather.3.cloned.1.call-done, bf16[3072,1536]{1,0:T(8,128)(2,1)} %all-gather.5.cloned.1.call-done, bf16[256,1536]{1,0:T(8,128)(2,1)} %param.5, s32[1536]{0:T(1024)S(1)} %fusion.5, s32[256]{0:T(256)} %param.7), kind=kOutput, calls=%fused_computation.7 | convolution fusion | flops 2418671616 | bytes 12590080 | tf_op jit(solution)/shard_map/dot_general | solution.py:25
  122.7 0.0 copy-done
  122.7 2.7 %convolution_convert_fusion = bf16[256,3072]{1,0:T(8,128)(2,1)S(1)} fusion(bf16[256,1536]{1,0:T(8,128)(2,1)S(1)} %fusion.4, bf16[3072,1536]{1,0:T(8,128)(2,1)S(1)} %copy-done), kind=kOutput, calls=%fused_computation.2 | convolution fusion | flops 2416705536 | bytes 11796480 | tf_op jit(solution)/shard_map/dot_general | solution.py:29
  125.4 1.6 copy.8
  127.0 0.0 copy-start.1
  127.0 0.0 reduce-scatter.7.cloned.1.call-update
  127.0 0.0 reduce-scatter.9.cloned.1.call-start
  127.1 1.3 copy-done.1
  128.4 5.1 %fusion = bf16[3072,1536]{0,1:T(8,128)(2,1)} fusion(bf16[256,1536]{1,0:T(8,128)(2,1)S(1)} %fusion.4, bf16[256,3072]{1,0:T(8,128)(2,1)S(1)} %copy-done.1), kind=kOutput, calls=%fused_computation.1 | convolution fusion | flops 2425356288 | bytes 11796480 | tf_op jit(solution)/shard_map/dot_general | solution.py:30
  133.5 12.8 %copy.10 = bf16[3072,1536]{1,0:T(8,128)(2,1)} copy(bf16[3072,1536]{0,1:T(8,128)(2,1)} %fusion) | data formatting | bytes 18874368
  146.3 0.0 reduce-scatter.9.cloned.1.call-update
  146.3 10.3 %reduce-scatter.7.cloned.1.call-done = bf16[384,256]{1,0:T(8,128)(2,1)} async-done(((bf16[3072,256]{1,0:T(8,128)(2,1)}), bf16[384,256]{1,0:T(8,128)(2,1)}) %reduce-scatter.7.cloned.1.call-update) | async-done | bytes 196624
  156.6 1.7 copy.9
  158.3 90.4 %reduce-scatter.9.cloned.1.call-done = bf16[192,1536]{1,0:T(8,128)(2,1)} async-done(((bf16[3072,1536]{1,0:T(8,128)(2,1)}), bf16[192,1536]{1,0:T(8,128)(2,1)}) %reduce-scatter.9.cloned.1.call-update) | async-done | bytes 589840
  (1 shorter events, 0.0 us)
Async XLA Ops:
  7.2 30.9 %all-gather.3.cloned.1.call-start = ((), (), s32[]{:S(2)}) async-start(), calls=%async_computation.2 | async-start | bytes 1769472 | tf_op jit(solution)/shard_map/all_gather | solution.py:17
  7.9 107.7 %all-gather.5.cloned.1.call-start = ((), (), s32[]{:S(2)}) async-start(), calls=%async_computation.3 | async-start | bytes 10027008 | tf_op jit(solution)/shard_map/all_gather | solution.py:20
  8.6 147.9 %reduce-scatter.7.cloned.1.call-start = ((), (), s32[]{:S(2)}) async-start(), calls=%async_computation.4 | async-start | bytes 1769472
  115.6 7.1 %copy-start = (bf16[3072,1536]{1,0:T(8,128)(2,1)S(1)}, bf16[3072,1536]{1,0:T(8,128)(2,1)}, u32[]{:S(2)}) copy-start(bf16[3072,1536]{1,0:T(8,128)(2,1)} %all-gather.5.cloned.1.call-done) | copy-start | bytes 28311556
  127.0 1.4 copy-start.1
  127.0 121.7 %reduce-scatter.9.cloned.1.call-start = ((), (), s32[]{:S(2)}) async-start(), calls=%async_computation.5 | async-start | bytes 10027008
Sparse Core Ops, SparseCore 0:
  9.7 28.2 all-gather.2
  40.2 75.3 all-gather.4
  127.2 29.3 reduce-scatter.6
  160.5 88.1 reduce-scatter.8
where the time goes:
time: 256 us; the launch traced here: 255 us
  waiting for transfers between devices  209 us (82%)
  local copies, waits for them, and re-layouts  17.4 us (7%)
  matrix products  14.9 us (6%)
  between operations  13.8 us (5%)
    unnamed x6, waiting for transfers between devices  102 us
    all_gather x1, waiting for transfers between devices, shards(): weights = lax.all_gather(up_weight, 'dp', axis=0, tiled=True)  77.6 us
    all_gather x1, waiting for transfers between devices, shards(): whole_x = lax.all_gather(activations, 'tensor', axis=1, tiled=True)  29.3 us
    unnamed x7, local copies, waits for them, and re-layouts  17.4 us
    dot_general x1, matrix products, shards(): preact = jnp.dot(whole_x, weights, preferred_element_type=jnp.float32)  7.12 us
  transfers between devices with their start and end apart: 4, of which 4 were waited for; matrix products, arithmetic and copies ran while one was open for 8% of the time, Pallas kernels for 0%

commit v1 on v0

v1 whole, which is shorter than its diff:
```python
import jax
import jax.numpy as jnp
from jax import lax
from jax.experimental import pallas as pl
from jax.experimental.pallas import tpu as pltpu
from jax.sharding import PartitionSpec as P

MESH = pl.DeviceIdType.MESH
F32 = jnp.float32
BF16 = jnp.bfloat16
TOK = 256
ROWS = 192
COLS = 384
HID = 1536
SCALE = 1.0 / 64.0
N_SEM = 160


def gray(j):
    return (0, 1, 3, 2)[j]


def kernel(
    x_ref, g_ref, w_ref, wid_ref, dx_ref, dw_ref,
    xb, wb, gb, gin, hid, sd, sr, vp, vm, ap, am, xr, dw, zvp, zvm, zap, zam, tot,
    ssem, rsem, lsem,
):
    dp, tensor = lax.axis_index("dp"), lax.axis_index("tensor")
    z, x = lax.div(dp, 4), lax.rem(dp, 4)
    y, c = lax.div(tensor, 2), lax.rem(tensor, 2)

    def ring(v, step):
        return lax.rem(v + step, 4)

    def device(dz=0, dx=0, dy=0, dc=0):
        return (
            ring(z, dz) * 4 + ring(x, dx),
            ring(y, dy) * 2 + lax.rem(c + dc, 2),
        )

    sites = {}

    def send(name, src, dst, **to):
        slot = len(sites)
        copy = pltpu.make_async_remote_copy(
            src_ref=src,
            dst_ref=dst,
            send_sem=ssem.at[slot],
            recv_sem=rsem.at[slot],
            device_id=device(**to),
            device_id_type=MESH,
        )
        copy.start()
        sites[name] = copy

    def arrived(name):
        sites[name].wait_recv()

    def token_rows(step):
        return pl.ds(pl.multiple_of(ring(x, step) * TOK, TOK), TOK)

    def token_half(step, half):
        return pl.ds(pl.multiple_of(ring(x, step) * TOK + half * 128, 128), 128)

    def weight_rows(dz, dx):
        return pl.ds(pl.multiple_of((ring(z, dz) * 4 + ring(x, dx)) * ROWS, ROWS), ROWS)

    def weight_half(dz, dx, half):
        start = (ring(z, dz) * 4 + ring(x, dx)) * ROWS + half * 96
        return pl.ds(pl.multiple_of(start, 96), 96)

    def cols_of(step):
        return pl.ds(pl.multiple_of(ring(x, step) * COLS, COLS), COLS)

    def feature(dy):
        return ring(y, dy) * 2 + c

    own_g = pltpu.make_async_copy(g_ref, gin, lsem.at[0])
    own_x = pltpu.make_async_copy(x_ref, xb.at[feature(0), token_rows(0)], lsem.at[1])
    own_w = pltpu.make_async_copy(w_ref.at[:, cols_of(0)], wb.at[weight_rows(0, 0)], lsem.at[2])
    own_g.start()
    own_x.start()
    own_w.start()

    partners = (
        dict(dx=1), dict(dx=3), dict(dx=2), dict(dy=1), dict(dy=3), dict(dz=1), dict(dz=3), dict(dc=1),
    )
    barrier = pltpu.get_barrier_semaphore()
    for to in partners:
        pl.semaphore_signal(barrier, inc=1, device_id=device(**to), device_id_type=MESH)
    with jax.named_scope("barrier"):
        pl.semaphore_wait(barrier, len(partners))

    def x_ref_or(j):
        return x_ref if j == 0 else xb.at[feature(0), token_rows(gray(j))]

    def y_send(j):
        dst = xb.at[feature(0), token_rows(gray(j))]
        send(f"yp{j}", x_ref_or(j), dst, dy=1)
        send(f"ym{j}", x_ref_or(j), dst, dy=3)
        send(f"s0{j}", x_ref_or(j), dst, dc=1)

    def y_forward(j):
        arrived(f"yp{j}")
        ref = xb.at[feature(3), token_half(gray(j), 0)]
        send(f"yfp{j}", ref, ref, dy=1)
        arrived(f"ym{j}")
        ref = xb.at[feature(1), token_half(gray(j), 1)]
        send(f"yfm{j}", ref, ref, dy=3)
        ref = xb.at[feature(3), token_rows(gray(j))]
        send(f"s1{j}", ref, ref, dc=1)
        ref = xb.at[feature(1), token_rows(gray(j))]
        send(f"s2{j}", ref, ref, dc=1)

    def y_last(j):
        arrived(f"yfp{j}")
        arrived(f"yfm{j}")
        ref = xb.at[feature(2), token_rows(gray(j))]
        send(f"s3{j}", ref, ref, dc=1)

    def tokens_ready(j):
        for part in range(4):
            arrived(f"s{part}{j}")

    def z_send(j):
        dst = wb.at[weight_rows(0, gray(j))]
        src = w_ref.at[:, cols_of(0)] if j == 0 else dst
        send(f"zp{j}", src, dst, dz=1)
        send(f"zm{j}", src, dst, dz=3)

    def z_forward(j):
        arrived(f"zp{j}")
        ref = wb.at[weight_half(3, gray(j), 0)]
        send(f"zfp{j}", ref, ref, dz=1)
        arrived(f"zm{j}")
        ref = wb.at[weight_half(1, gray(j), 1)]
        send(f"zfm{j}", ref, ref, dz=3)

    def z_last(j):
        arrived(f"zfp{j}")
        arrived(f"zfm{j}")

    def x_send(step):
        send(f"x{step}", x_ref, xb.at[feature(0), token_rows(0)], dx=step)

    def w_send(step):
        send(f"w{step}", w_ref.at[:, cols_of(step)], wb.at[weight_rows(0, 0)], dx=step)

    def g_send(step):
        send(f"g{step}", gin.at[:, cols_of(step)], gb.at[token_rows(0)], dx=step)

    x_send(1)
    x_send(3)
    y_send(0)
    z_send(0)
    w_send(1)
    w_send(3)
    w_send(2)
    x_send(2)

    own_g.wait()
    with jax.named_scope("mask"):
        for half in range(2):
            rows = pl.ds(half * 128, 128)
            width = jnp.broadcast_to(wid_ref[half : half + 1, :], (128, 128)).T
            keep = jnp.where(width > tensor, 1.0, 0.0).astype(BF16)
            for part in range(HID // 128):
                lanes = pl.ds(part * 128, 128)
                gin[rows, lanes] = gin[rows, lanes] * keep
    put_g = pltpu.make_async_copy(gin.at[:, cols_of(0)], gb.at[token_rows(0)], lsem.at[0])
    put_g.start()
    own_x.wait()
    own_w.wait()

    with jax.named_scope("z_forward0"):
        z_forward(0)
    with jax.named_scope("x_arrive13"):
        arrived("x3")
        y_send(1)
        arrived("x1")
        y_send(2)
    with jax.named_scope("y_forward0"):
        y_forward(0)
    with jax.named_scope("w_arrive13"):
        arrived("w3")
        z_send(1)
        arrived("w1")
        z_send(2)
    g_send(1)
    g_send(3)
    with jax.named_scope("z_last0"):
        z_last(0)
    with jax.named_scope("y_last0"):
        y_last(0)
    with jax.named_scope("w_arrive2"):
        arrived("w2")
        z_send(3)
    with jax.named_scope("x_arrive2"):
        arrived("x2")
        y_send(3)
    g_send(2)
    with jax.named_scope("z_forward1"):
        z_forward(1)
        z_forward(2)
    with jax.named_scope("y_forward1"):
        y_forward(1)
        y_forward(2)
    with jax.named_scope("z_last1"):
        z_last(1)
        z_last(2)
    with jax.named_scope("z_forward3"):
        z_forward(3)
    with jax.named_scope("y_last1"):
        y_last(1)
        y_last(2)
    with jax.named_scope("z_last3"):
        z_last(3)

    def hidden(j):
        tokens_ready(j)
        if j == 0:
            put_g.wait()
        else:
            arrived(f"g{(None, 3, 1, 2)[j]}")
        rows = token_rows(gray(j))
        whole = jnp.concatenate([xb[k, rows, :] for k in range(8)], axis=1)
        preact = jnp.dot(whole, wb[...], preferred_element_type=F32)
        slope = 2.0 * jnp.maximum(preact, 0.0)
        hid[rows, :] = (gb[rows, :].astype(F32) * slope).astype(BF16)

    def input_parts(j):
        h = hid[token_rows(gray(j)), :]
        for d in (2, 1, 3, 0):
            rows = pl.ds(pl.multiple_of(ring(y, d) * 768, 768), 768)
            part = lax.dot_general(
                h, wb[rows, :], (((1,), (1,)), ((), ())), preferred_element_type=F32
            ).astype(BF16)
            sd[j, d, 0] = part[:, :COLS]
            sd[j, d, 1] = part[:, COLS:]
            send(f"p{d}{j}", sd.at[j, d, 1 - c], sr.at[j, d], dc=1)

    def add_pair(j, d):
        arrived(f"p{d}{j}")
        total = sd[j, d, c].astype(F32) + sr[j, d].astype(F32)
        sd[j, d, c] = total.astype(BF16)

    top, low = pl.ds(0, 128), pl.ds(128, 128)

    def input_sends(j):
        add_pair(j, 2)
        send(f"vp{j}", sd.at[j, 2, c, top], vp.at[j], dy=1)
        send(f"vm{j}", sd.at[j, 2, c, low], vm.at[j], dy=3)
        add_pair(j, 1)
        send(f"apl{j}", sd.at[j, 1, c, low], ap.at[j, low], dy=1)
        add_pair(j, 3)
        send(f"amt{j}", sd.at[j, 3, c, top], am.at[j, top], dy=3)

    def input_via(j):
        arrived(f"vp{j}")
        sd[j, 1, c, top] = (sd[j, 1, c, top].astype(F32) + vp[j].astype(F32)).astype(BF16)
        send(f"apt{j}", sd.at[j, 1, c, top], ap.at[j, top], dy=1)
        arrived(f"vm{j}")
        sd[j, 3, c, low] = (sd[j, 3, c, low].astype(F32) + vm[j].astype(F32)).astype(BF16)
        send(f"aml{j}", sd.at[j, 3, c, low], am.at[j, low], dy=3)

    def input_total(j):
        for name in ("p0", "apl", "amt", "apt", "aml"):
            arrived(f"{name}{j}")
        return (
            sd[j, 0, c].astype(F32)
            + sr[j, 0].astype(F32)
            + ap[j].astype(F32)
            + am[j].astype(F32)
        )

    def input_last(j):
        sd[j, 0, c] = input_total(j).astype(BF16)
        step = gray(j)
        send(f"xr{step}", sd.at[j, 0, c], xr.at[step - 1], dx=step)

    def weight_parts(d):
        for half in range(2):
            part = lax.dot_general(
                xb[ring(z, d) * 2 + half],
                hid[...],
                (((0,), (0,)), ((), ())),
                preferred_element_type=F32,
            ).astype(BF16)
            for piece in range(2):
                place = lax.rem(half * 2 + piece - x + 7, 4)
                rows = pl.ds(pl.multiple_of(place * 96, 96), 96)
                first = piece * ROWS
                dw[d, 0, rows, :] = part[first : first + 96]
                dw[d, 1, rows, :] = part[first + 96 : first + ROWS]

    def weight_via():
        arrived("zvp")
        arrived("zvm")
        for q in range(4):
            rows = pl.ds(q * 96, 96)
            dw[1, 0, rows] = (dw[1, 0, rows].astype(F32) + zvp[rows].astype(F32)).astype(BF16)
            send(f"zapc{q}", dw.at[1, 0, rows], zap.at[0, rows], dz=1)
            dw[3, 1, rows] = (dw[3, 1, rows].astype(F32) + zvm[rows].astype(F32)).astype(BF16)
            send(f"zamc{q}", dw.at[3, 1, rows], zam.at[1, rows], dz=3)

    def weight_last(q):
        if q == 0:
            arrived("zapd")
            arrived("zamd")
        arrived(f"zapc{q}")
        arrived(f"zamc{q}")
        rows = pl.ds(q * 96, 96)
        for half in range(2):
            total = (
                dw[0, half, rows].astype(F32)
                + zap[half, rows].astype(F32)
                + zam[half, rows].astype(F32)
            )
            tot[q, pl.ds(half * 96, 96)] = (total * SCALE).astype(BF16)
        if q < 3:
            send(f"t{q}", tot.at[q], dw_ref.at[:, cols_of(0)], dx=q + 1)

    with jax.named_scope("hidden0"):
        hidden(0)
    with jax.named_scope("hidden1"):
        hidden(1)
    with jax.named_scope("input_parts1"):
        input_parts(1)
        input_sends(1)
    with jax.named_scope("hidden2"):
        hidden(2)
    with jax.named_scope("input_via1"):
        input_via(1)
    with jax.named_scope("input_parts2"):
        input_parts(2)
        input_sends(2)
    with jax.named_scope("y_forward3"):
        y_forward(3)
        y_last(3)
    with jax.named_scope("hidden3"):
        hidden(3)
    with jax.named_scope("weight_parts2"):
        weight_parts(2)
        send("zvp", dw.at[2, 0], zvp, dz=1)
        send("zvm", dw.at[2, 1], zvm, dz=3)
    with jax.named_scope("input_via2"):
        input_via(2)
    with jax.named_scope("input_parts3"):
        input_parts(3)
        input_sends(3)
    with jax.named_scope("weight_parts13"):
        weight_parts(1)
        send("zapd", dw.at[1, 1], zap.at[1], dz=1)
        weight_parts(3)
        send("zamd", dw.at[3, 0], zam.at[0], dz=3)
    with jax.named_scope("input_last1"):
        input_last(1)
    with jax.named_scope("input_via3"):
        input_via(3)
    with jax.named_scope("input_parts0"):
        input_parts(0)
        input_sends(0)
    with jax.named_scope("weight_via"):
        weight_via()
    with jax.named_scope("weight_parts0"):
        weight_parts(0)
    with jax.named_scope("input_last2"):
        input_last(2)
    with jax.named_scope("input_via0"):
        input_via(0)
    with jax.named_scope("weight_last0"):
        weight_last(0)
    with jax.named_scope("input_last3"):
        input_last(3)
    with jax.named_scope("weight_last1"):
        weight_last(1)
        weight_last(2)
        weight_last(3)
        put_w = pltpu.make_async_copy(tot.at[3], dw_ref.at[:, cols_of(0)], lsem.at[1])
        put_w.start()
    with jax.named_scope("input_final"):
        total = input_total(0)
        for step in (1, 3, 2):
            arrived(f"xr{step}")
            total = total + xr[step - 1].astype(F32)
        dx_ref[...] = total.astype(BF16)
    with jax.named_scope("ends"):
        for q in range(3):
            arrived(f"t{q}")
        put_w.wait()
        for copy in sites.values():
            copy.wait_send()


def shards(activations, act_grad, up_weight, width_steps):
    any_space = pl.BlockSpec(memory_space=pl.ANY)
    vmem = pl.BlockSpec(memory_space=pltpu.VMEM)

    def buffer(*shape):
        return pltpu.VMEM(shape, BF16)

    return pl.pallas_call(
        kernel,
        out_shape=(
            jax.ShapeDtypeStruct((TOK, COLS), BF16),
            jax.ShapeDtypeStruct((ROWS, HID), BF16),
        ),
        in_specs=[any_space, any_space, any_space, vmem],
        out_specs=(vmem, any_space),
        scratch_shapes=[
            buffer(8, 4 * TOK, COLS),
            buffer(16 * ROWS, COLS),
            buffer(4 * TOK, COLS),
            buffer(TOK, HID),
            buffer(4 * TOK, COLS),
            buffer(4, 4, 2, TOK, COLS),
            buffer(4, 4, TOK, COLS),
            buffer(4, 128, COLS),
            buffer(4, 128, COLS),
            buffer(4, TOK, COLS),
            buffer(4, TOK, COLS),
            buffer(3, TOK, COLS),
            buffer(4, 2, 384, COLS),
            buffer(384, COLS),
            buffer(384, COLS),
            buffer(2, 384, COLS),
            buffer(2, 384, COLS),
            buffer(4, ROWS, COLS),
            pltpu.SemaphoreType.DMA((N_SEM,)),
            pltpu.SemaphoreType.DMA((N_SEM,)),
            pltpu.SemaphoreType.DMA((3,)),
        ],
        compiler_params=pltpu.CompilerParams(
            collective_id=0, has_side_effects=True, vmem_limit_bytes=50 * 2**20
        ),
        cost_estimate=pl.CostEstimate(
            flops=3 * 2 * 1024 * 3072 * 384, bytes_accessed=4 * 2**20, transcendentals=0
        ),
        name="elastic_up_backward",
    )(activations, act_grad, up_weight, width_steps.reshape(2, 128))


def solution(mesh):
    placed = (P("dp", "tensor"), P("dp", "tensor"), P("dp", "tensor"), P("dp"))
    return jax.shard_map(
        shards,
        mesh=mesh,
        in_specs=placed,
        out_specs=(P("dp", "tensor"), P("dp", "tensor")),
        check_vma=False,
    )
```

time: 256 us -> 99.8 us (0.39)
  waiting for transfers between devices: 209 us -> 0 us
  Pallas kernels: 0 us -> 93.6 us
  matrix products: 14.9 us -> 0 us
  between operations: 13.8 us -> 0.65 us
  local copies, waits for them, and re-layouts: 17.4 us -> 5.29 us
    all_gather x2 -> x0, waiting for transfers between devices: 107 us -> none  [the longest x1 77.6 us: shards(): weights = lax.all_gather(up_weight, 'dp', axis=0, tiled=True)]
    unnamed x6 -> x0, waiting for transfers between devices: 102 us -> none
    pallas_call x0 -> x1, Pallas kernels: none -> 93.6 us  [shards(): pl.pallas_call(kernel, out_shape=(jax.ShapeDtypeStruct((TOK, COLS), BF16)...]
    dot_general x3 -> x0, matrix products: 14.9 us -> none  [the longest x1 7.12 us: shards(): preact = jnp.dot(whole_x, weights, preferred_element_type=jnp.float32)]
    unnamed x7 -> x10, local copies, waits for them, and re-layouts: 17.4 us -> 5.29 us
  transfers between devices with their start and end apart: 4 -> 0, of which waited for: 4 -> 0; matrix products, arithmetic and copies ran while one was open for 8% -> 0% of each run, Pallas kernels for 0% -> 0%
where the time goes in v1:
time: 99.8 us; the launch traced here: 99.5 us
  Pallas kernels  93.6 us (94%)
  local copies, waits for them, and re-layouts  5.29 us (5%)
    pallas_call x1, Pallas kernels, shards(): pl.pallas_call(kernel, out_shape=(jax.ShapeDtypeStruct((TOK, COLS), BF16)...  93.6 us
    unnamed x10, local copies, waits for them, and re-layouts  5.29 us

profile of v1, /device:TPU:1, one launch (start us, length us, event | category | flops | bytes accessed | tf_op | source)
XLA Modules:
  0.0 99.5 jit_solution(5277862426980969850)
XLA Ops:
  0.6 0.0 copy-start.3
  0.6 0.7 copy-done.3
  1.3 0.0 copy-start
  1.3 1.1 %copy-done = bf16[256,1536]{1,0:T(8,128)(2,1)S(1)} copy-done((bf16[256,1536]{1,0:T(8,128)(2,1)S(1)}, bf16[256,1536]{1,0:T(8,128)(2,1)}, u32[]{:S(2)}) %copy-start) | copy-done | bytes 786456
  2.4 0.0 copy-start.1
  2.4 1.1 %copy-done.1 = bf16[192,1536]{1,0:T(8,128)(2,1)S(1)} copy-done((bf16[192,1536]{1,0:T(8,128)(2,1)S(1)}, bf16[192,1536]{1,0:T(8,128)(2,1)}, u32[]{:S(2)}) %copy-start.1) | copy-done | bytes 589848
  3.5 0.0 copy-start.2
  3.5 0.9 copy-done.2
  4.4 93.6 %elastic_up_backward.1 = (bf16[256,384]{1,0:T(8,128)(2,1)S(1)}, bf16[192,1536]{1,0:T(8,128)(2,1)S(1)}) custom-call(bf16[256,384]{1,0:T(8,128)(2,1)S(1)} %copy-done.2, bf16[256,1536]{1,0:T(8,128)(2,1)S(1)} %copy-done, bf16[192,1536]{1,0:T(8,128)(2,1)S(1)} %copy-done.1, s32[2,128]{1,0:T(2,128)S(1)} %bitcast.1), custom_call_target="tpu_custom_call" | custom-call | flops 7247757312 | bytes 4194304 | tf_op jit(solution)/shard_map/elastic_up_backward/pallas_call | solution.py:402
  98.0 0.7 copy.8
  98.7 0.8 copy.9
Async XLA Ops:
  0.6 0.7 copy-start.3
  1.3 1.1 %copy-start = (bf16[256,1536]{1,0:T(8,128)(2,1)S(1)}, bf16[256,1536]{1,0:T(8,128)(2,1)}, u32[]{:S(2)}) copy-start(bf16[256,1536]{1,0:T(8,128)(2,1)} %g_ref.1) | copy-start | bytes 2359300
  2.4 1.1 %copy-start.1 = (bf16[192,1536]{1,0:T(8,128)(2,1)S(1)}, bf16[192,1536]{1,0:T(8,128)(2,1)}, u32[]{:S(2)}) copy-start(bf16[192,1536]{1,0:T(8,128)(2,1)} %w_ref.1) | copy-start | bytes 1769476
  3.5 0.9 copy-start.2

commit v2 on v0

v2 whole, which is shorter than its diff:
```python
import jax
import jax.numpy as jnp
from jax import lax
from jax.experimental import pallas as pl
from jax.experimental.pallas import tpu as pltpu
from jax.sharding import PartitionSpec as P

MESH = pl.DeviceIdType.MESH
F32 = jnp.float32
BF16 = jnp.bfloat16
TOK = 256
HALF = 128
ROWS = 192
COLS = 384
HID = 1536
SCALE = 1.0 / 64.0
N_SEM = 168

STEP = (0, 1, 3, 2)
FROM = (0, 3, 1, 2)
PLACE = (2, 0, 1, 3)

ORDER = (
    "mask", "g13", "g2", "zfp0", "zfm0", "yfp0", "yfm0", "wa2", "wa1", "zdm0", "zdp0", "xa2", "xa1", "zl0",
    "zfp2", "zfm2", "xb2", "xb1", "zdp2", "zdm2", "yfp2", "zfp1", "zfm1", "wa3", "yfp1", "zdp1", "zdm1",
    "zl2", "xa3", "yfm2", "zl1", "xb3", "yfm1", "zfp3", "zfm3", "zdp3", "zdm3", "zl3", "wr2", "P0", "yfp3",
    "yfm3", "PA", "IA1", "IA3", "P3", "D21", "IA0", "IB2", "IA2", "E21", "D20", "D10", "D31", "R1", "E20",
    "IB3", "E10", "E31", "IB1", "D11", "R2", "D30", "IB0", "E11", "D01", "E30", "ZVm", "S0", "ZVp", "D00",
    "E01", "R3", "E00", "Vm", "Vp", "ZL0", "ZL1", "ZL2", "R0", "ZL3", "RF",
)

def kernel(
    x_ref, g_ref, w_ref, wid_ref, dx_ref, dw_ref,
    xb, wb, gb, gin, wid, hid, sd, qb, vp, vm, ap, am, rb, xr, own,
    dwp, dwr, dws, zvp, zvm, zap, zam, tot, ssem, rsem, lsem,
):
    dp, tensor = lax.axis_index("dp"), lax.axis_index("tensor")
    z, x = lax.div(dp, 4), lax.rem(dp, 4)
    y, c = lax.div(tensor, 2), lax.rem(tensor, 2)
    other = 1 - c

    def ring(v, step):
        return lax.rem(v + step, 4)

    def device(dz=0, dx=0, dy=0, dc=0):
        return (
            ring(z, dz) * 4 + ring(x, dx),
            ring(y, dy) * 2 + (other if dc else c),
        )

    sites = {}

    def send(name, src, dst, **to):
        slot = len(sites)
        copy = pltpu.make_async_remote_copy(
            src_ref=src,
            dst_ref=dst,
            send_sem=ssem.at[slot],
            recv_sem=rsem.at[slot],
            device_id=device(**to),
            device_id_type=MESH,
        )
        copy.start()
        sites[name] = copy

    def arrived(*names):
        for name in names:
            sites[name].wait_recv()

    def place(j):
        return pl.ds(PLACE[j] * HALF, HALF)

    def chunk(dy, core):
        return ring(y, dy) * 2 + core

    def half_of(core):
        return pl.ds(pl.multiple_of(core * HALF, HALF), HALF)

    def weight_rows(dz, dx):
        return pl.ds(pl.multiple_of((ring(z, dz) * 4 + ring(x, dx)) * ROWS, ROWS), ROWS)

    def weight_half(dz, dx, half):
        start = (ring(z, dz) * 4 + ring(x, dx)) * ROWS + half * 96
        return pl.ds(pl.multiple_of(start, 96), 96)

    def sub_block(step):
        return pl.ds(pl.multiple_of(ring(x, step) * COLS, COLS), COLS)

    own_cols = pl.ds(pl.multiple_of(c * COLS, COLS), COLS)

    own_w = pltpu.make_async_copy(
        w_ref.at[:, sub_block(0)], wb.at[weight_rows(0, 0), own_cols], lsem.at[2]
    )
    own_x = pltpu.make_async_copy(
        x_ref.at[half_of(c)], xb.at[chunk(0, c), place(0)], lsem.at[1]
    )
    own_g = pltpu.make_async_copy(g_ref, gin, lsem.at[0])
    own_wid = pltpu.make_async_copy(wid_ref, wid, lsem.at[3])
    own_wid.start()
    own_g.start()
    own_x.start()
    own_w.start()
    put_g = pltpu.make_async_copy(
        gin.at[half_of(c), sub_block(0)], gb.at[place(0), own_cols], lsem.at[0]
    )
    put_w = pltpu.make_async_copy(tot.at[3], dw_ref.at[:, sub_block(0)], lsem.at[1])

    partners = (
        dict(dx=1), dict(dx=3), dict(dx=2), dict(dy=1), dict(dy=3), dict(dz=1), dict(dz=3), dict(dc=1),
        dict(dx=1, dc=1), dict(dx=3, dc=1), dict(dx=2, dc=1), dict(dy=1, dc=1), dict(dy=3, dc=1),
    )
    barrier = pltpu.get_barrier_semaphore()
    for to in partners:
        pl.semaphore_signal(barrier, inc=1, device_id=device(**to), device_id_type=MESH)
    pl.semaphore_wait(barrier, len(partners))

    tasks = {}

    def task(name, *args):
        def enter(step):
            tasks[name] = lambda: step(*args)
            return step

        return enter

    def x_send(step, kind):
        core, dc = (c, 0) if kind == "s" else (other, 1)
        j = FROM[STEP.index(step)]
        dst = xb.at[chunk(0, c), place(STEP.index(j))]
        send(f"x{step}{kind}", x_ref.at[half_of(core)], dst, dx=step, dc=dc)

    def y_send(j, name, kind):
        dy = 1 if name == "yp" else 3
        if j == 0:
            core, dc = (c, 0) if kind == "s" else (other, 1)
            send(f"{name}0{kind}", x_ref.at[half_of(core)], xb.at[chunk(0, c), place(0)], dy=dy, dc=dc)
        else:
            ref = xb.at[chunk(0, c if kind == "s" else other), place(j)]
            send(f"{name}{j}{kind}", ref, ref, dy=dy)

    def x_arrive(j, kind):
        arrived(f"x{FROM[j]}{kind}")
        y_send(j, "yp", kind)
        y_send(j, "ym", kind)

    def y_forward_up(j):
        arrived(f"yp{j}s")
        ref = xb.at[chunk(3, c), place(j)]
        send(f"yfp{j}", ref, ref, dy=1)

    def y_forward_down(j):
        arrived(f"ym{j}o")
        ref = xb.at[chunk(1, other), place(j)]
        send(f"yfm{j}", ref, ref, dy=3)

    def w_send(step):
        dst = wb.at[weight_rows(0, 0), own_cols]
        send(f"w{step}", w_ref.at[:, sub_block(step)], dst, dx=step)

    def z_send(j, name, half):
        dst = wb.at[weight_half(0, STEP[j], half), own_cols]
        src = w_ref.at[pl.ds(half * 96, 96), sub_block(0)] if j == 0 else dst
        send(f"{name}{j}{'ab'[half]}", src, dst, dz=1 if name == "zp" else 3)

    def w_arrive(j):
        arrived(f"w{FROM[j]}")
        z_send(j, "zp", 0)
        z_send(j, "zm", 1)
        z_send(j, "zp", 1)
        z_send(j, "zm", 0)
        w_pair(f"ws{j}", 0, j)

    def w_pair(name, dz, j):
        dst = wb.at[weight_rows(dz, STEP[j]), own_cols]
        src = w_ref.at[:, sub_block(0)] if name == "ws0" else dst
        send(name, src, dst, dc=1)

    def z_forward_up(j):
        arrived(f"zp{j}a")
        ref = wb.at[weight_half(3, STEP[j], 0), own_cols]
        send(f"zfp{j}", ref, ref, dz=1)

    def z_forward_down(j):
        arrived(f"zm{j}b")
        ref = wb.at[weight_half(1, STEP[j], 1), own_cols]
        send(f"zfm{j}", ref, ref, dz=3)

    def z_whole_up(j):
        arrived(f"zp{j}b")
        w_pair(f"d1{j}", 3, j)

    def z_whole_down(j):
        arrived(f"zm{j}a")
        w_pair(f"d3{j}", 1, j)

    def z_across(j):
        arrived(f"zfp{j}", f"zfm{j}")
        w_pair(f"d2{j}", 2, j)

    @task("wr2")
    def weights_ready():
        own_w.wait()
        for j in range(4):
            arrived(f"ws{j}", f"d1{j}", f"d3{j}", f"d2{j}")

    def g_send(step, kind):
        core, dc = (c, 0) if kind == "s" else (other, 1)
        j = FROM[STEP.index(step)]
        dst = gb.at[place(STEP.index(j)), own_cols]
        send(f"g{step}{kind}", gin.at[half_of(core), sub_block(step)], dst, dx=step, dc=dc)

    @task("mask")
    def mask():
        own_wid.wait()
        own_g.wait()
        for half in range(2):
            rows = pl.ds(half * 128, 128)
            width = jnp.broadcast_to(wid[half : half + 1, :], (128, 128)).T
            keep = jnp.where(width > tensor, 1.0, 0.0).astype(BF16)
            for part in range(HID // 128):
                lanes = pl.ds(part * 128, 128)
                gin[rows, lanes] = gin[rows, lanes] * keep
        put_g.start()
        send("gs", gin.at[half_of(other), sub_block(0)], gb.at[place(0), own_cols], dc=1)

    @task("g13")
    def g_near():
        g_send(1, "s")
        g_send(3, "s")
        g_send(1, "o")
        g_send(3, "o")

    @task("g2")
    def g_across():
        g_send(2, "s")
        g_send(2, "o")

    for j in range(4):
        if j:
            task(f"xa{j}", j, "s")(x_arrive)
            task(f"xb{j}", j, "o")(x_arrive)
            task(f"wa{j}", j)(w_arrive)
        task(f"yfp{j}", j)(y_forward_up)
        task(f"yfm{j}", j)(y_forward_down)
        task(f"zfp{j}", j)(z_forward_up)
        task(f"zfm{j}", j)(z_forward_down)
        task(f"zdp{j}", j)(z_whole_up)
        task(f"zdm{j}", j)(z_whole_down)
        task(f"zl{j}", j)(z_across)

    def hidden(*places):
        for j in places:
            arrived(f"yp{j}o", f"ym{j}s", f"yfp{j}", f"yfm{j}")
            if j == 0:
                own_x.wait()
                put_g.wait()
                arrived("xs", "gs")
            else:
                arrived(f"g{FROM[j]}s", f"g{FROM[j]}o")
        rows = pl.ds(PLACE[places[0]] * HALF, HALF * len(places))
        whole = jnp.concatenate([xb[k, rows, :] for k in range(8)], axis=1)
        preact = jnp.dot(whole, wb[...], preferred_element_type=F32)
        slope = 2.0 * jnp.maximum(preact, 0.0)
        hid[rows, :] = (gb[rows, :].astype(F32) * slope).astype(BF16)

    task("PA", 1, 2)(hidden)
    task("P0", 0)(hidden)
    task("P3", 3)(hidden)

    first, second = pl.ds(0, 128), pl.ds(128, 128)
    upper, lower = pl.ds(0, 64), pl.ds(64, 64)

    def input_part(b, d):
        rows = pl.ds(pl.multiple_of(ring(y, d) * 768, 768), 768)
        sd[b, d] = lax.dot_general(
            hid[pl.ds(b * 256, 256), :], wb[rows, :], (((1,), (1,)), ((), ())), preferred_element_type=F32
        ).astype(BF16)
        if d == 2 and b == 0:
            send("q1", sd.at[0, 2, first], qb.at[0], dx=1)
            send("q3", sd.at[0, 2, second], qb.at[2], dx=3)
        elif d == 2:
            send("q2", sd.at[1, 2, second], qb.at[1], dx=2)
        elif d == 1 and b == 0:
            send("a11", sd.at[0, 1, first], ap.at[0], dy=1)
            send("a12", sd.at[0, 1, second], ap.at[1], dy=1)
        elif d == 3 and b == 0:
            send("a31", sd.at[0, 3, first], am.at[0], dy=3)
            send("a32", sd.at[0, 3, second], am.at[1], dy=3)
        elif d == 1:
            send("a13", sd.at[1, 1, second], ap.at[3], dy=1)
            send("a10l", sd.at[1, 1, lower], ap.at[2, lower], dy=1)
        elif d == 3:
            send("a33", sd.at[1, 3, second], am.at[3], dy=3)
            send("a30t", sd.at[1, 3, upper], am.at[2, upper], dy=3)

    for b in range(2):
        for d in range(4):
            task(f"I{'AB'[b]}{d}", b, d)(input_part)

    @task("S0")
    def across_total():
        arrived("q1", "q3", "q2")
        total = sd[1, 2, first].astype(F32)
        for slot in range(3):
            total = total + qb[slot].astype(F32)
        sd[1, 2, first] = total.astype(BF16)
        send("vp", sd.at[1, 2, upper], vp, dy=1)
        send("vm", sd.at[1, 2, lower], vm, dy=3)

    @task("Vp")
    def via_up():
        arrived("vp")
        sd[1, 1, upper] = (sd[1, 1, upper].astype(F32) + vp[...].astype(F32)).astype(BF16)
        send("a10t", sd.at[1, 1, upper], ap.at[2, upper], dy=1)

    @task("Vm")
    def via_down():
        arrived("vm")
        sd[1, 3, lower] = (sd[1, 3, lower].astype(F32) + vm[...].astype(F32)).astype(BF16)
        send("a30l", sd.at[1, 3, lower], am.at[2, lower], dy=3)

    def input_total(j):
        if j == 0:
            arrived("a10l", "a10t", "a30t", "a30l")
        else:
            arrived(f"a1{j}", f"a3{j}")
        at, rows = PLACE[j], (first, second)[PLACE[j] % 2]
        total = sd[at // 2, 0, rows].astype(F32) + ap[at].astype(F32) + am[at].astype(F32)
        total = total.astype(BF16)
        rb[at, 0] = total[:, :COLS]
        rb[at, 1] = total[:, COLS:]
        if j == 0:
            own[c] = rb[at, c]
            send("xro", rb.at[at, other], own.at[c], dc=1)
        else:
            step = STEP[j]
            send(f"xr{step}s", rb.at[at, c], xr.at[step - 1, c], dx=step)
            send(f"xr{step}o", rb.at[at, other], xr.at[step - 1, c], dx=step, dc=1)

    for j in range(4):
        task(f"R{j}", j)(input_total)

    @task("RF")
    def input_final():
        arrived("xr1s", "xr1o", "xr3s", "xr3o", "xr2s", "xr2o", "xro")
        for half in range(2):
            total = own[half].astype(F32)
            for slot in range(3):
                total = total + xr[slot, half].astype(F32)
            dx_ref[pl.ds(half * HALF, HALF), :] = total.astype(BF16)

    def weight_part(d, h):
        part = lax.dot_general(
            xb[ring(z, d) * 2 + h], hid[...], (((0,), (0,)), ((), ())), preferred_element_type=F32
        ).astype(BF16)
        dwp[d, h, 0] = part[:, :COLS]
        dwp[d, h, 1] = part[:, COLS:]
        send(f"e{d}{h}", dwp.at[d, h, other], dwr.at[d, h], dc=1)

    def weight_pair(d, h):
        arrived(f"e{d}{h}")
        total = (dwp[d, h, c].astype(F32) + dwr[d, h].astype(F32)).astype(BF16)
        for p in range(2):
            at = lax.rem(h * 2 + p - x + 7, 4)
            rows = pl.ds(pl.multiple_of(at * 96, 96), 96)
            dws[d, 0, rows] = total[p * ROWS : p * ROWS + 96]
            dws[d, 1, rows] = total[p * ROWS + 96 : p * ROWS + ROWS]
            if d == 2:
                send(f"zvp{h}{p}", dws.at[2, 0, rows], zvp.at[rows], dz=1)
                send(f"zvm{h}{p}", dws.at[2, 1, rows], zvm.at[rows], dz=3)
            elif d == 1:
                send(f"zdp{h}{p}", dws.at[1, 1, rows], zap.at[1, rows], dz=1)
            elif d == 3:
                send(f"zdm{h}{p}", dws.at[3, 0, rows], zam.at[0, rows], dz=3)

    for d in range(4):
        for h in range(2):
            task(f"D{d}{h}", d, h)(weight_part)
            task(f"E{d}{h}", d, h)(weight_pair)

    def sub_rows(q):
        return pl.ds(q * 96, 96)

    @task("ZVp")
    def weight_via_up():
        arrived("zvp00", "zvp01", "zvp10", "zvp11")
        for q in range(4):
            rows = sub_rows(q)
            dws[1, 0, rows] = (dws[1, 0, rows].astype(F32) + zvp[rows].astype(F32)).astype(BF16)
            send(f"zcp{q}", dws.at[1, 0, rows], zap.at[0, rows], dz=1)

    @task("ZVm")
    def weight_via_down():
        arrived("zvm00", "zvm01", "zvm10", "zvm11")
        for q in range(4):
            rows = sub_rows(q)
            dws[3, 1, rows] = (dws[3, 1, rows].astype(F32) + zvm[rows].astype(F32)).astype(BF16)
            send(f"zcm{q}", dws.at[3, 1, rows], zam.at[1, rows], dz=3)

    def weight_last(q):
        if q == 0:
            for tail in ("00", "01", "10", "11"):
                arrived("zdp" + tail, "zdm" + tail)
        arrived(f"zcp{q}", f"zcm{q}")
        rows = sub_rows(q)
        for half in range(2):
            total = (
                dws[0, half, rows].astype(F32) + zap[half, rows].astype(F32) + zam[half, rows].astype(F32)
            )
            tot[q, pl.ds(half * 96, 96)] = (total * SCALE).astype(BF16)
        if q < 3:
            send(f"t{q}", tot.at[q], dw_ref.at[:, sub_block(0)], dx=q + 1)
        else:
            put_w.start()

    for q in range(4):
        task(f"ZL{q}", q)(weight_last)

    w_send(1)
    w_send(3)
    x_send(1, "s")
    x_send(3, "s")
    y_send(0, "yp", "s")
    y_send(0, "ym", "o")
    z_send(0, "zp", 0)
    z_send(0, "zm", 1)
    x_send(1, "o")
    x_send(3, "o")
    y_send(0, "yp", "o")
    y_send(0, "ym", "s")
    z_send(0, "zp", 1)
    z_send(0, "zm", 0)
    w_pair("ws0", 0, 0)
    send("xs", x_ref.at[half_of(other)], xb.at[chunk(0, c), place(0)], dc=1)
    w_send(2)
    x_send(2, "s")
    x_send(2, "o")
    for name in ORDER:
        tasks[name]()
    arrived("t0", "t1", "t2")
    put_w.wait()
    for copy in sites.values():
        copy.wait_send()


def shards(activations, act_grad, up_weight, width_steps):
    any_space = pl.BlockSpec(memory_space=pl.ANY)
    vmem = pl.BlockSpec(memory_space=pltpu.VMEM)

    def buffer(*shape):
        return pltpu.VMEM(shape, BF16)

    return pl.pallas_call(
        kernel,
        out_shape=(
            jax.ShapeDtypeStruct((TOK, COLS), BF16),
            jax.ShapeDtypeStruct((ROWS, HID), BF16),
        ),
        in_specs=[any_space, any_space, any_space, any_space],
        out_specs=(vmem, any_space),
        scratch_shapes=[
            buffer(8, 4 * HALF, COLS),
            buffer(16 * ROWS, 2 * COLS),
            buffer(4 * HALF, 2 * COLS),
            buffer(TOK, HID),
            pltpu.VMEM((2, 128), jnp.int32),
            buffer(4 * HALF, 2 * COLS),
            buffer(2, 4, 2 * HALF, 2 * COLS),
            buffer(3, HALF, 2 * COLS),
            buffer(64, 2 * COLS),
            buffer(64, 2 * COLS),
            buffer(4, HALF, 2 * COLS),
            buffer(4, HALF, 2 * COLS),
            buffer(4, 2, HALF, COLS),
            buffer(3, 2, HALF, COLS),
            buffer(2, HALF, COLS),
            buffer(4, 2, 2, 384, COLS),
            buffer(4, 2, 384, COLS),
            buffer(4, 2, 384, COLS),
            buffer(384, COLS),
            buffer(384, COLS),
            buffer(2, 384, COLS),
            buffer(2, 384, COLS),
            buffer(4, ROWS, COLS),
            pltpu.SemaphoreType.DMA((N_SEM,)),
            pltpu.SemaphoreType.DMA((N_SEM,)),
            pltpu.SemaphoreType.DMA((4,)),
        ],
        compiler_params=pltpu.CompilerParams(
            collective_id=0, has_side_effects=True, vmem_limit_bytes=60 * 2**20
        ),
        cost_estimate=pl.CostEstimate(
            flops=3 * 2 * 512 * 3072 * 768, bytes_accessed=4 * 2**20, transcendentals=0
        ),
        name="elastic_up_backward",
    )(activations, act_grad, up_weight, width_steps.reshape(2, 128))


def solution(mesh):
    placed = (P("dp", "tensor"), P("dp", "tensor"), P("dp", "tensor"), P("dp"))
    return jax.shard_map(
        shards,
        mesh=mesh,
        in_specs=placed,
        out_specs=(P("dp", "tensor"), P("dp", "tensor")),
        check_vma=False,
    )
```

time: 256 us -> 77.2 us (0.30)
  waiting for transfers between devices: 209 us -> 0 us
  Pallas kernels: 0 us -> 72.9 us
  matrix products: 14.9 us -> 0 us
  local copies, waits for them, and re-layouts: 17.4 us -> 3.54 us
  between operations: 13.8 us -> 0.64 us
    all_gather x2 -> x0, waiting for transfers between devices: 107 us -> none  [the longest x1 77.6 us: shards(): weights = lax.all_gather(up_weight, 'dp', axis=0, tiled=True)]
    unnamed x6 -> x0, waiting for transfers between devices: 102 us -> none
    pallas_call x0 -> x1, Pallas kernels: none -> 72.9 us  [shards(): pl.pallas_call(kernel, out_shape=(jax.ShapeDtypeStruct((TOK, COLS), BF16)...]
    dot_general x3 -> x0, matrix products: 14.9 us -> none  [the longest x1 7.12 us: shards(): preact = jnp.dot(whole_x, weights, preferred_element_type=jnp.float32)]
    unnamed x7 -> x2, local copies, waits for them, and re-layouts: 17.4 us -> 3.54 us
  transfers between devices with their start and end apart: 4 -> 0, of which waited for: 4 -> 0; matrix products, arithmetic and copies ran while one was open for 8% -> 0% of each run, Pallas kernels for 0% -> 0%
where the time goes in v2:
time: 77.2 us; the launch traced here: 77.1 us
  Pallas kernels  72.9 us (94%)
  local copies, waits for them, and re-layouts  3.54 us (5%)
    pallas_call x1, Pallas kernels, shards(): pl.pallas_call(kernel, out_shape=(jax.ShapeDtypeStruct((TOK, COLS), BF16)...  72.9 us
    unnamed x2, local copies, waits for them, and re-layouts  3.54 us

profile of v2, /device:TPU:1, one launch (start us, length us, event | category | flops | bytes accessed | tf_op | source)
XLA Modules:
  0.0 77.1 jit_solution(30100234490814249)
XLA Ops:
  0.6 72.9 %elastic_up_backward.1 = (bf16[256,384]{1,0:T(8,128)(2,1)}, bf16[192,1536]{1,0:T(8,128)(2,1)}) custom-call(bf16[256,384]{1,0:T(8,128)(2,1)} %x_ref.1, bf16[256,1536]{1,0:T(8,128)(2,1)} %g_ref.1, bf16[192,1536]{1,0:T(8,128)(2,1)} %w_ref.1, s32[2,128]{1,0:T(2,128)} %bitcast.1), custom_call_target="tpu_custom_call" | custom-call | flops 7247757312 | bytes 4194304 | tf_op jit(solution)/shard_map/elastic_up_backward/pallas_call | solution.py:453
  73.5 1.6 %copy.8 = bf16[256,384]{1,0:T(8,128)(2,1)} copy(bf16[256,384]{1,0:T(8,128)(2,1)} %get-tuple-element.4) | data formatting | bytes 393216
  75.1 1.9 %copy.9 = bf16[192,1536]{1,0:T(8,128)(2,1)} copy(bf16[192,1536]{1,0:T(8,128)(2,1)} %get-tuple-element.5) | data formatting | bytes 1179648

commit v3 on v2

--- a/solution.py
+++ b/solution.py
@@ -14,24 +14,27 @@
 COLS = 384
 HID = 1536
 SCALE = 1.0 / 64.0
-N_SEM = 168
+N_SEM = 176
 
 STEP = (0, 1, 3, 2)
 FROM = (0, 3, 1, 2)
 PLACE = (2, 0, 1, 3)
+SLOT = (0, 1, 3, 2)
+SUB = (2, 1, 3, 0)
 
 ORDER = (
-    "mask", "g13", "g2", "zfp0", "zfm0", "yfp0", "yfm0", "wa2", "wa1", "zdm0", "zdp0", "xa2", "xa1", "zl0",
-    "zfp2", "zfm2", "xb2", "xb1", "zdp2", "zdm2", "yfp2", "zfp1", "zfm1", "wa3", "yfp1", "zdp1", "zdm1",
-    "zl2", "xa3", "yfm2", "zl1", "xb3", "yfm1", "zfp3", "zfm3", "zdp3", "zdm3", "zl3", "wr2", "P0", "yfp3",
-    "yfm3", "PA", "IA1", "IA3", "P3", "D21", "IA0", "IB2", "IA2", "E21", "D20", "D10", "D31", "R1", "E20",
-    "IB3", "E10", "E31", "IB1", "D11", "R2", "D30", "IB0", "E11", "D01", "E30", "ZVm", "S0", "ZVp", "D00",
-    "E01", "R3", "E00", "Vm", "Vp", "ZL0", "ZL1", "ZL2", "R0", "ZL3", "RF",
+    "xa2", "yfp0", "xb1", "zfm0", "zfp0", "wa2", "yfm0", "zdm0", "w2s", "wa1", "xa1", "xa3", "mask", "zfp2",
+    "yfp2", "xb3", "zfm2", "xy3", "xy1", "zdp0", "wa3", "g13", "zdm2", "zl0", "yfm1", "zfp1", "zfm1", "xb2",
+    "zdm1", "zdp2", "zfm3", "zfp3", "zdp1", "yfp3", "g2", "yfm3", "zl2", "zdp3", "zdm3", "zl1", "wr1", "Pa0",
+    "zl3", "PaA", "wr2", "PbA", "IA1", "IA3", "Pa3", "Pb0", "Pb3", "D20", "IA2", "D31", "IB2", "D10", "IA0",
+    "E20", "D21", "D11", "E31", "D30", "E21", "D00", "IB1", "E10", "IB3", "E11", "sent", "E30", "R1", "Zc0",
+    "E00", "Zd0", "R2", "D01", "V3p", "E01", "V3m", "S0", "Zd1", "Zd2", "Zc1", "ZL0", "IB0", "Zc2", "R3",
+    "Vm", "Zd3", "ZL1", "Vp", "ZL2", "Zc3", "R0", "RF", "ZL3",
 )
 
 def kernel(
     x_ref, g_ref, w_ref, wid_ref, dx_ref, dw_ref,
-    xb, wb, gb, gin, wid, hid, sd, qb, vp, vm, ap, am, rb, xr, own,
+    xb, wb, gb, gin, wid, acc, hid, sd, qb, vp, vm, vp3, vm3, ap, am, rb, xr, own, out,
     dwp, dwr, dws, zvp, zvm, zap, zam, tot, ssem, rsem, lsem,
 ):
     dp, tensor = lax.axis_index("dp"), lax.axis_index("tensor")
@@ -63,9 +66,13 @@
         copy.start()
         sites[name] = copy
 
+    taken = set()
+
     def arrived(*names):
         for name in names:
-            sites[name].wait_recv()
+            if name not in taken:
+                taken.add(name)
+                sites[name].wait_recv()
 
     def place(j):
         return pl.ds(PLACE[j] * HALF, HALF)
@@ -77,10 +84,10 @@
         return pl.ds(pl.multiple_of(core * HALF, HALF), HALF)
 
     def weight_rows(dz, dx):
-        return pl.ds(pl.multiple_of((ring(z, dz) * 4 + ring(x, dx)) * ROWS, ROWS), ROWS)
+        return pl.ds(pl.multiple_of(SLOT[dz] * 768 + ring(x, dx) * ROWS, ROWS), ROWS)
 
     def weight_half(dz, dx, half):
-        start = (ring(z, dz) * 4 + ring(x, dx)) * ROWS + half * 96
+        start = SLOT[dz] * 768 + ring(x, dx) * ROWS + half * 96
         return pl.ds(pl.multiple_of(start, 96), 96)
 
     def sub_block(step):
@@ -104,6 +111,7 @@
         gin.at[half_of(c), sub_block(0)], gb.at[place(0), own_cols], lsem.at[0]
     )
     put_w = pltpu.make_async_copy(tot.at[3], dw_ref.at[:, sub_block(0)], lsem.at[1])
+    put_x = pltpu.make_async_copy(out, dx_ref, lsem.at[2])
 
     partners = (
         dict(dx=1), dict(dx=3), dict(dx=2), dict(dy=1), dict(dy=3), dict(dz=1), dict(dz=3), dict(dc=1),
@@ -139,9 +147,30 @@
             send(f"{name}{j}{kind}", ref, ref, dy=dy)
 
     def x_arrive(j, kind):
-        arrived(f"x{FROM[j]}{kind}")
-        y_send(j, "yp", kind)
-        y_send(j, "ym", kind)
+        if j < 3:
+            arrived(f"x{FROM[j]}{kind}")
+        else:
+            arrived("xf1" if kind == "s" else "xf3")
+        if j == 2 and kind == "s":
+            at = chunk(0, c)
+            send("xf1", xb.at[at, place(2)], xb.at[at, place(3)], dx=1)
+        if j == 1 and kind == "o":
+            at = chunk(0, other)
+            send("xf3", xb.at[at, place(1)], xb.at[at, place(3)], dx=3)
+        for name in ("yp", "ym") if kind == "s" else ("ym", "yp"):
+            y_send(j, name, kind)
+
+    @task("xy3")
+    def across_back():
+        arrived("yfp0")
+        at = chunk(2, c)
+        send("xy3s", xb.at[at, place(0)], xb.at[at, place(1)], dx=3)
+
+    @task("xy1")
+    def across_on():
+        arrived("yfm0")
+        at = chunk(2, other)
+        send("xy1o", xb.at[at, place(0)], xb.at[at, place(2)], dx=1)
 
     def y_forward_up(j):
         arrived(f"yp{j}s")
@@ -158,9 +187,12 @@
         send(f"w{step}", w_ref.at[:, sub_block(step)], dst, dx=step)
 
     def z_send(j, name, half):
-        dst = wb.at[weight_half(0, STEP[j], half), own_cols]
-        src = w_ref.at[pl.ds(half * 96, 96), sub_block(0)] if j == 0 else dst
-        send(f"{name}{j}{'ab'[half]}", src, dst, dz=1 if name == "zp" else 3)
+        to = 1 if name == "zp" else 3
+        src = wb.at[weight_half(0, STEP[j], half), own_cols]
+        if j == 0:
+            src = w_ref.at[pl.ds(half * 96, 96), sub_block(0)]
+        dst = wb.at[weight_half(4 - to, STEP[j], half), own_cols]
+        send(f"{name}{j}{'ab'[half]}", src, dst, dz=to)
 
     def w_arrive(j):
         arrived(f"w{FROM[j]}")
@@ -177,13 +209,13 @@
 
     def z_forward_up(j):
         arrived(f"zp{j}a")
-        ref = wb.at[weight_half(3, STEP[j], 0), own_cols]
-        send(f"zfp{j}", ref, ref, dz=1)
+        src = wb.at[weight_half(3, STEP[j], 0), own_cols]
+        send(f"zfp{j}", src, wb.at[weight_half(2, STEP[j], 0), own_cols], dz=1)
 
     def z_forward_down(j):
         arrived(f"zm{j}b")
-        ref = wb.at[weight_half(1, STEP[j], 1), own_cols]
-        send(f"zfm{j}", ref, ref, dz=3)
+        src = wb.at[weight_half(1, STEP[j], 1), own_cols]
+        send(f"zfm{j}", src, wb.at[weight_half(2, STEP[j], 1), own_cols], dz=3)
 
     def z_whole_up(j):
         arrived(f"zp{j}b")
@@ -197,11 +229,20 @@
         arrived(f"zfp{j}", f"zfm{j}")
         w_pair(f"d2{j}", 2, j)
 
-    @task("wr2")
-    def weights_ready():
+    @task("w2s")
+    def w_across():
+        w_send(2)
+
+    @task("wr1")
+    def weights_near():
         own_w.wait()
         for j in range(4):
-            arrived(f"ws{j}", f"d1{j}", f"d3{j}", f"d2{j}")
+            arrived(f"ws{j}", f"d1{j}", f"d3{j}")
+
+    @task("wr2")
+    def weights_across():
+        for j in range(4):
+            arrived(f"d2{j}")
 
     def g_send(step, kind):
         core, dc = (c, 0) if kind == "s" else (other, 1)
@@ -248,38 +289,64 @@
         task(f"zdm{j}", j)(z_whole_down)
         task(f"zl{j}", j)(z_across)
 
-    def hidden(*places):
+    def features(dz, rows):
+        return [xb[ring(z, dz) * 2 + h, rows, :] for h in range(2)]
+
+    def batch(places):
+        return pl.ds(PLACE[places[0]] * HALF, HALF * len(places))
+
+    def hidden_near(*places):
         for j in places:
-            arrived(f"yp{j}o", f"ym{j}s", f"yfp{j}", f"yfm{j}")
+            arrived(f"yp{j}o", f"ym{j}s")
+            if j == 1:
+                arrived("yp1s", "xy3s")
+            else:
+                arrived(f"yfp{j}")
+            if j == 2:
+                arrived("ym2o", "xy1o")
+            else:
+                arrived(f"yfm{j}")
             if j == 0:
                 own_x.wait()
+                arrived("xs")
+        rows = batch(places)
+        part = jnp.concatenate(features(0, rows) + features(1, rows) + features(3, rows), axis=1)
+        acc[rows, :] = jnp.dot(part, wb[pl.ds(0, 2304), :], preferred_element_type=F32)
+
+    def hidden_last(*places):
+        for j in places:
+            if j == 0:
                 put_g.wait()
-                arrived("xs", "gs")
+                arrived("gs")
             else:
                 arrived(f"g{FROM[j]}s", f"g{FROM[j]}o")
-        rows = pl.ds(PLACE[places[0]] * HALF, HALF * len(places))
-        whole = jnp.concatenate([xb[k, rows, :] for k in range(8)], axis=1)
-        preact = jnp.dot(whole, wb[...], preferred_element_type=F32)
+        rows = batch(places)
+        part = jnp.concatenate(features(2, rows), axis=1)
+        preact = acc[rows, :] + jnp.dot(part, wb[pl.ds(2304, 768), :], preferred_element_type=F32)
         slope = 2.0 * jnp.maximum(preact, 0.0)
         hid[rows, :] = (gb[rows, :].astype(F32) * slope).astype(BF16)
 
-    task("PA", 1, 2)(hidden)
-    task("P0", 0)(hidden)
-    task("P3", 3)(hidden)
+    for name, places in (("A", (1, 2)), ("0", (0,)), ("3", (3,))):
+        task("Pa" + name, *places)(hidden_near)
+        task("Pb" + name, *places)(hidden_last)
 
     first, second = pl.ds(0, 128), pl.ds(128, 128)
     upper, lower = pl.ds(0, 64), pl.ds(64, 64)
+    upper3, lower3 = pl.ds(128, 64), pl.ds(192, 64)
 
     def input_part(b, d):
-        rows = pl.ds(pl.multiple_of(ring(y, d) * 768, 768), 768)
+        dz = lax.rem(y + d - z + 4, 4)
+        slot = dz + lax.div(dz, 2) - 2 * lax.div(dz, 3)
+        rows = pl.ds(pl.multiple_of(slot * 768, 768), 768)
         sd[b, d] = lax.dot_general(
             hid[pl.ds(b * 256, 256), :], wb[rows, :], (((1,), (1,)), ((), ())), preferred_element_type=F32
         ).astype(BF16)
         if d == 2 and b == 0:
             send("q1", sd.at[0, 2, first], qb.at[0], dx=1)
-            send("q3", sd.at[0, 2, second], qb.at[2], dx=3)
+            send("q3", sd.at[0, 2, second], qb.at[1], dx=3)
         elif d == 2:
-            send("q2", sd.at[1, 2, second], qb.at[1], dx=2)
+            send("vp3", sd.at[1, 2, upper3], vp3, dy=1)
+            send("vm3", sd.at[1, 2, lower3], vm3, dy=3)
         elif d == 1 and b == 0:
             send("a11", sd.at[0, 1, first], ap.at[0], dy=1)
             send("a12", sd.at[0, 1, second], ap.at[1], dy=1)
@@ -287,10 +354,10 @@
             send("a31", sd.at[0, 3, first], am.at[0], dy=3)
             send("a32", sd.at[0, 3, second], am.at[1], dy=3)
         elif d == 1:
-            send("a13", sd.at[1, 1, second], ap.at[3], dy=1)
+            send("a13l", sd.at[1, 1, lower3], ap.at[3, lower], dy=1)
             send("a10l", sd.at[1, 1, lower], ap.at[2, lower], dy=1)
         elif d == 3:
-            send("a33", sd.at[1, 3, second], am.at[3], dy=3)
+            send("a33t", sd.at[1, 3, upper3], am.at[3, upper], dy=3)
             send("a30t", sd.at[1, 3, upper], am.at[2, upper], dy=3)
 
     for b in range(2):
@@ -299,29 +366,32 @@
 
     @task("S0")
     def across_total():
-        arrived("q1", "q3", "q2")
+        arrived("q1", "q3")
         total = sd[1, 2, first].astype(F32)
-        for slot in range(3):
+        for slot in range(2):
             total = total + qb[slot].astype(F32)
         sd[1, 2, first] = total.astype(BF16)
         send("vp", sd.at[1, 2, upper], vp, dy=1)
         send("vm", sd.at[1, 2, lower], vm, dy=3)
 
-    @task("Vp")
-    def via_up():
-        arrived("vp")
-        sd[1, 1, upper] = (sd[1, 1, upper].astype(F32) + vp[...].astype(F32)).astype(BF16)
-        send("a10t", sd.at[1, 1, upper], ap.at[2, upper], dy=1)
-
-    @task("Vm")
-    def via_down():
-        arrived("vm")
-        sd[1, 3, lower] = (sd[1, 3, lower].astype(F32) + vm[...].astype(F32)).astype(BF16)
-        send("a30l", sd.at[1, 3, lower], am.at[2, lower], dy=3)
+    def via_up(name, came, rows, to, at):
+        arrived(name)
+        sd[1, 1, rows] = (sd[1, 1, rows].astype(F32) + came[...].astype(F32)).astype(BF16)
+        send(to, sd.at[1, 1, rows], ap.at[at, upper], dy=1)
+
+    def via_down(name, came, rows, to, at):
+        arrived(name)
+        sd[1, 3, rows] = (sd[1, 3, rows].astype(F32) + came[...].astype(F32)).astype(BF16)
+        send(to, sd.at[1, 3, rows], am.at[at, lower], dy=3)
+
+    task("Vp", "vp", vp, upper, "a10t", 2)(via_up)
+    task("Vm", "vm", vm, lower, "a30l", 2)(via_down)
+    task("V3p", "vp3", vp3, upper3, "a13t", 3)(via_up)
+    task("V3m", "vm3", vm3, lower3, "a33l", 3)(via_down)
 
     def input_total(j):
-        if j == 0:
-            arrived("a10l", "a10t", "a30t", "a30l")
+        if j in (0, 3):
+            arrived(f"a1{j}l", f"a1{j}t", f"a3{j}t", f"a3{j}l")
         else:
             arrived(f"a1{j}", f"a3{j}")
         at, rows = PLACE[j], (first, second)[PLACE[j] % 2]
@@ -347,7 +417,8 @@
             total = own[half].astype(F32)
             for slot in range(3):
                 total = total + xr[slot, half].astype(F32)
-            dx_ref[pl.ds(half * HALF, HALF), :] = total.astype(BF16)
+            out[pl.ds(half * HALF, HALF), :] = total.astype(BF16)
+        put_x.start()
 
     def weight_part(d, h):
         part = lax.dot_general(
@@ -361,17 +432,14 @@
         arrived(f"e{d}{h}")
         total = (dwp[d, h, c].astype(F32) + dwr[d, h].astype(F32)).astype(BF16)
         for p in range(2):
-            at = lax.rem(h * 2 + p - x + 7, 4)
+            step = lax.rem(h * 2 + p - x + 4, 4)
+            at = lax.rem(lax.rem(3 * step + 3, 5), 4)
             rows = pl.ds(pl.multiple_of(at * 96, 96), 96)
             dws[d, 0, rows] = total[p * ROWS : p * ROWS + 96]
             dws[d, 1, rows] = total[p * ROWS + 96 : p * ROWS + ROWS]
             if d == 2:
-                send(f"zvp{h}{p}", dws.at[2, 0, rows], zvp.at[rows], dz=1)
-                send(f"zvm{h}{p}", dws.at[2, 1, rows], zvm.at[rows], dz=3)
-            elif d == 1:
-                send(f"zdp{h}{p}", dws.at[1, 1, rows], zap.at[1, rows], dz=1)
-            elif d == 3:
-                send(f"zdm{h}{p}", dws.at[3, 0, rows], zam.at[0, rows], dz=3)
+                via_copy("zvp", at, rows).start()
+                via_copy("zvm", at, rows).start()
 
     for d in range(4):
         for h in range(2):
@@ -381,27 +449,39 @@
     def sub_rows(q):
         return pl.ds(q * 96, 96)
 
-    @task("ZVp")
-    def weight_via_up():
-        arrived("zvp00", "zvp01", "zvp10", "zvp11")
+    via_slots = {}
+
+    def via_copy(name, at, rows):
+        up = name == "zvp"
+        return pltpu.make_async_remote_copy(
+            src_ref=dws.at[2, 0 if up else 1, rows],
+            dst_ref=(zvp if up else zvm).at[rows],
+            send_sem=ssem.at[via_slots[name] + at],
+            recv_sem=rsem.at[via_slots[name] + at],
+            device_id=device(dz=1 if up else 3),
+            device_id_type=MESH,
+        )
+
+    for name in ("zvp", "zvm"):
+        via_slots[name] = len(sites)
         for q in range(4):
-            rows = sub_rows(q)
-            dws[1, 0, rows] = (dws[1, 0, rows].astype(F32) + zvp[rows].astype(F32)).astype(BF16)
-            send(f"zcp{q}", dws.at[1, 0, rows], zap.at[0, rows], dz=1)
-
-    @task("ZVm")
-    def weight_via_down():
-        arrived("zvm00", "zvm01", "zvm10", "zvm11")
-        for q in range(4):
-            rows = sub_rows(q)
-            dws[3, 1, rows] = (dws[3, 1, rows].astype(F32) + zvm[rows].astype(F32)).astype(BF16)
-            send(f"zcm{q}", dws.at[3, 1, rows], zam.at[1, rows], dz=3)
+            sites[f"{name}{q}"] = via_copy(name, q, sub_rows(q))
+
+    def weight_direct(q):
+        rows = sub_rows(q)
+        send(f"zdp{q}", dws.at[1, 1, rows], zap.at[1, rows], dz=1)
+        send(f"zdm{q}", dws.at[3, 0, rows], zam.at[0, rows], dz=3)
+
+    def weight_via(q):
+        arrived(f"zvp{q}", f"zvm{q}")
+        rows = sub_rows(q)
+        dws[1, 0, rows] = (dws[1, 0, rows].astype(F32) + zvp[rows].astype(F32)).astype(BF16)
+        send(f"zcp{q}", dws.at[1, 0, rows], zap.at[0, rows], dz=1)
+        dws[3, 1, rows] = (dws[3, 1, rows].astype(F32) + zvm[rows].astype(F32)).astype(BF16)
+        send(f"zcm{q}", dws.at[3, 1, rows], zam.at[1, rows], dz=3)
 
     def weight_last(q):
-        if q == 0:
-            for tail in ("00", "01", "10", "11"):
-                arrived("zdp" + tail, "zdm" + tail)
-        arrived(f"zcp{q}", f"zcm{q}")
+        arrived(f"zdp{q}", f"zdm{q}", f"zcp{q}", f"zcm{q}")
         rows = sub_rows(q)
         for half in range(2):
             total = (
@@ -409,64 +489,86 @@
             )
             tot[q, pl.ds(half * 96, 96)] = (total * SCALE).astype(BF16)
         if q < 3:
-            send(f"t{q}", tot.at[q], dw_ref.at[:, sub_block(0)], dx=q + 1)
+            send(f"t{q}", tot.at[q], dw_ref.at[:, sub_block(0)], dx=SUB[q])
         else:
             put_w.start()
 
     for q in range(4):
+        task(f"Zd{q}", q)(weight_direct)
+        task(f"Zc{q}", q)(weight_via)
         task(f"ZL{q}", q)(weight_last)
 
+    left = set()
+
+    @task("sent")
+    def early_sends():
+        for name, copy in list(sites.items()):
+            if not name.startswith("zv"):
+                left.add(name)
+                copy.wait_send()
+
+    x_send(1, "s")
+    x_send(3, "o")
     w_send(1)
     w_send(3)
-    x_send(1, "s")
+    x_send(1, "o")
     x_send(3, "s")
     y_send(0, "yp", "s")
     y_send(0, "ym", "o")
     z_send(0, "zp", 0)
     z_send(0, "zm", 1)
-    x_send(1, "o")
-    x_send(3, "o")
     y_send(0, "yp", "o")
     y_send(0, "ym", "s")
     z_send(0, "zp", 1)
     z_send(0, "zm", 0)
     w_pair("ws0", 0, 0)
     send("xs", x_ref.at[half_of(other)], xb.at[chunk(0, c), place(0)], dc=1)
-    w_send(2)
-    x_send(2, "s")
-    x_send(2, "o")
     for name in ORDER:
         tasks[name]()
+    for name, copy in sites.items():
+        if name not in left:
+            copy.wait_send()
     arrived("t0", "t1", "t2")
     put_w.wait()
-    for copy in sites.values():
-        copy.wait_send()
+    put_x.wait()
+
+
+def hand_on(a_ref, b_ref, a_out, b_out, sem):
+    first = pltpu.make_async_copy(a_ref, a_out, sem.at[0])
+    second = pltpu.make_async_copy(b_ref, b_out, sem.at[1])
+    second.start()
+    first.start()
+    first.wait()
+    second.wait()
 
 
 def shards(activations, act_grad, up_weight, width_steps):
     any_space = pl.BlockSpec(memory_space=pl.ANY)
-    vmem = pl.BlockSpec(memory_space=pltpu.VMEM)
 
     def buffer(*shape):
         return pltpu.VMEM(shape, BF16)
 
-    return pl.pallas_call(
+    results = (
+        jax.ShapeDtypeStruct((TOK, COLS), BF16),
+        jax.ShapeDtypeStruct((ROWS, HID), BF16),
+    )
+    input_grad, weight_grad = pl.pallas_call(
         kernel,
-        out_shape=(
-            jax.ShapeDtypeStruct((TOK, COLS), BF16),
-            jax.ShapeDtypeStruct((ROWS, HID), BF16),
-        ),
+        out_shape=results,
         in_specs=[any_space, any_space, any_space, any_space],
-        out_specs=(vmem, any_space),
+        out_specs=(any_space, any_space),
         scratch_shapes=[
             buffer(8, 4 * HALF, COLS),
             buffer(16 * ROWS, 2 * COLS),
             buffer(4 * HALF, 2 * COLS),
             buffer(TOK, HID),
             pltpu.VMEM((2, 128), jnp.int32),
+            pltpu.VMEM((4 * HALF, 2 * COLS), F32),
             buffer(4 * HALF, 2 * COLS),
             buffer(2, 4, 2 * HALF, 2 * COLS),
-            buffer(3, HALF, 2 * COLS),
+            buffer(2, HALF, 2 * COLS),
+            buffer(64, 2 * COLS),
+            buffer(64, 2 * COLS),
             buffer(64, 2 * COLS),
             buffer(64, 2 * COLS),
             buffer(4, HALF, 2 * COLS),
@@ -474,6 +576,7 @@
             buffer(4, 2, HALF, COLS),
             buffer(3, 2, HALF, COLS),
             buffer(2, HALF, COLS),
+            buffer(TOK, COLS),
             buffer(4, 2, 2, 384, COLS),
             buffer(4, 2, 384, COLS),
             buffer(4, 2, 384, COLS),
@@ -494,6 +597,15 @@
         ),
         name="elastic_up_backward",
     )(activations, act_grad, up_weight, width_steps.reshape(2, 128))
+    return pl.pallas_call(
+        hand_on,
+        out_shape=results,
+        in_specs=[any_space, any_space],
+        out_specs=(any_space, any_space),
+        scratch_shapes=[pltpu.SemaphoreType.DMA((2,))],
+        compiler_params=pltpu.CompilerParams(vmem_limit_bytes=60 * 2**20),
+        name="hand_on",
+    )(input_grad, weight_grad)
 
 
 def solution(mesh):

time: 77.2 us -> 96.4 us (1.25)
  Pallas kernels: 72.9 us -> 95.7 us
  local copies, waits for them, and re-layouts: 3.54 us -> 0 us
    pallas_call x1 -> x2, Pallas kernels: 72.9 us -> 95.7 us  [the longest x1 70.7 us: shards(): pl.pallas_call(kernel, out_shape=results, in_specs=[any_space, any_space,...]
    unnamed x2 -> x0, local copies, waits for them, and re-layouts: 3.54 us -> none
where the time goes in v3:
time: 96.4 us; the launch traced here: 96.3 us
  Pallas kernels  95.7 us (99%)
    pallas_call x1, Pallas kernels, shards(): pl.pallas_call(kernel, out_shape=results, in_specs=[any_space, any_space,...  70.7 us
    pallas_call x1, Pallas kernels, shards(): pl.pallas_call(hand_on, out_shape=results, in_specs=[any_space, any_space...  24.9 us

profile of v3, /device:TPU:1, one launch (start us, length us, event | category | flops | bytes accessed | tf_op | source)
XLA Modules:
  0.0 96.3 jit_solution(5732929338382379389)
XLA Ops:
  0.6 70.7 %elastic_up_backward.1 = (bf16[256,384]{1,0:T(8,128)(2,1)}, bf16[192,1536]{1,0:T(8,128)(2,1)}) custom-call(bf16[256,384]{1,0:T(8,128)(2,1)} %x_ref.1, bf16[256,1536]{1,0:T(8,128)(2,1)} %g_ref.1, bf16[192,1536]{1,0:T(8,128)(2,1)} %w_ref.1, s32[2,128]{1,0:T(2,128)} %bitcast.1), custom_call_target="tpu_custom_call" | custom-call | flops 7247757312 | bytes 4194304 | tf_op jit(solution)/shard_map/elastic_up_backward/pallas_call | solution.py:555
  71.4 24.9 %hand_on.1 = (bf16[256,384]{1,0:T(8,128)(2,1)}, bf16[192,1536]{1,0:T(8,128)(2,1)}) custom-call(bf16[256,384]{1,0:T(8,128)(2,1)} %get-tuple-element.4.a_ref, bf16[192,1536]{1,0:T(8,128)(2,1)} %get-tuple-element.5.b_ref), custom_call_target="tpu_custom_call" | custom-call | tf_op jit(solution)/shard_map/hand_on/pallas_call | solution.py:600

commit v4 on v3

--- a/solution.py
+++ b/solution.py
@@ -498,14 +498,12 @@
         task(f"Zc{q}", q)(weight_via)
         task(f"ZL{q}", q)(weight_last)
 
-    left = set()
+    left = []
 
     @task("sent")
     def early_sends():
-        for name, copy in list(sites.items()):
-            if not name.startswith("zv"):
-                left.add(name)
-                copy.wait_send()
+        for name in left:
+            sites[name].wait_send()
 
     x_send(1, "s")
     x_send(3, "o")
@@ -524,6 +522,8 @@
     w_pair("ws0", 0, 0)
     send("xs", x_ref.at[half_of(other)], xb.at[chunk(0, c), place(0)], dc=1)
     for name in ORDER:
+        if name == "PbA":
+            left.extend(n for n in sites if n[:2] != "zv")
         tasks[name]()
     for name, copy in sites.items():
         if name not in left:
@@ -533,13 +533,18 @@
     put_x.wait()
 
 
-def hand_on(a_ref, b_ref, a_out, b_out, sem):
-    first = pltpu.make_async_copy(a_ref, a_out, sem.at[0])
-    second = pltpu.make_async_copy(b_ref, b_out, sem.at[1])
-    second.start()
-    first.start()
-    first.wait()
-    second.wait()
+def hand_on(a_ref, b_ref, a_out, b_out, a_buf, b_buf, sems):
+    parts = [(b_ref.at[pl.ds(k * 96, 96)], b_buf.at[pl.ds(k * 96, 96)], b_out.at[pl.ds(k * 96, 96)]) for k in range(2)]
+    parts.append((a_ref, a_buf, a_out))
+    loads = [pltpu.make_async_copy(src, buf, sems.at[0, k]) for k, (src, buf, _) in enumerate(parts)]
+    stores = [pltpu.make_async_copy(buf, dst, sems.at[1, k]) for k, (_, buf, dst) in enumerate(parts)]
+    for copy in loads:
+        copy.start()
+    for load, store in zip(loads, stores):
+        load.wait()
+        store.start()
+    for copy in stores:
+        copy.wait()
 
 
 def shards(activations, act_grad, up_weight, width_steps):
@@ -555,7 +560,7 @@
     input_grad, weight_grad = pl.pallas_call(
         kernel,
         out_shape=results,
-        in_specs=[any_space, any_space, any_space, any_space],
+        in_specs=[any_space] * 4,
         out_specs=(any_space, any_space),
         scratch_shapes=[
             buffer(8, 4 * HALF, COLS),
@@ -600,9 +605,9 @@
     return pl.pallas_call(
         hand_on,
         out_shape=results,
-        in_specs=[any_space, any_space],
+        in_specs=[any_space] * 2,
         out_specs=(any_space, any_space),
-        scratch_shapes=[pltpu.SemaphoreType.DMA((2,))],
+        scratch_shapes=[buffer(TOK, COLS), buffer(ROWS, HID), pltpu.SemaphoreType.DMA((2, 3))],
         compiler_params=pltpu.CompilerParams(vmem_limit_bytes=60 * 2**20),
         name="hand_on",
     )(input_grad, weight_grad)

time: 96.4 us -> 71.4 us (0.74)
  Pallas kernels: 95.7 us -> 70.6 us
    pallas_call x2, Pallas kernels: 95.7 us -> 70.6 us  [the longest x1 68.7 us: shards(): pl.pallas_call(kernel, out_shape=results, in_specs=[any_space] * 4, out_s...]
where the time goes in v4:
time: 71.4 us; the launch traced here: 71.2 us
  Pallas kernels  70.6 us (99%)
    pallas_call x1, Pallas kernels, shards(): pl.pallas_call(kernel, out_shape=results, in_specs=[any_space] * 4, out_s...  68.7 us
    pallas_call x1, Pallas kernels, shards(): pl.pallas_call(hand_on, out_shape=results, in_specs=[any_space] * 2, out_...  1.89 us

profile of v4, /device:TPU:1, one launch (start us, length us, event | category | flops | bytes accessed | tf_op | source)
XLA Modules:
  0.0 71.2 jit_solution(5221073446404273417)
XLA Ops:
  0.6 68.7 %elastic_up_backward.1 = (bf16[256,384]{1,0:T(8,128)(2,1)}, bf16[192,1536]{1,0:T(8,128)(2,1)}) custom-call(bf16[256,384]{1,0:T(8,128)(2,1)} %x_ref.1, bf16[256,1536]{1,0:T(8,128)(2,1)} %g_ref.1, bf16[192,1536]{1,0:T(8,128)(2,1)} %w_ref.1, s32[2,128]{1,0:T(2,128)} %bitcast.1), custom_call_target="tpu_custom_call" | custom-call | flops 7247757312 | bytes 4194304 | tf_op jit(solution)/shard_map/elastic_up_backward/pallas_call | solution.py:560
  69.3 1.9 %hand_on.1 = (bf16[256,384]{1,0:T(8,128)(2,1)}, bf16[192,1536]{1,0:T(8,128)(2,1)}) custom-call(bf16[256,384]{1,0:T(8,128)(2,1)} %get-tuple-element.4.a_ref, bf16[192,1536]{1,0:T(8,128)(2,1)} %get-tuple-element.5.b_ref), custom_call_target="tpu_custom_call" | custom-call | tf_op jit(solution)/shard_map/hand_on/pallas_call | solution.py:605

commit v5 on v4

--- a/solution.py
+++ b/solution.py
@@ -23,18 +23,18 @@
 SUB = (2, 1, 3, 0)
 
 ORDER = (
-    "xa2", "yfp0", "xb1", "zfm0", "zfp0", "wa2", "yfm0", "zdm0", "w2s", "wa1", "xa1", "xa3", "mask", "zfp2",
-    "yfp2", "xb3", "zfm2", "xy3", "xy1", "zdp0", "wa3", "g13", "zdm2", "zl0", "yfm1", "zfp1", "zfm1", "xb2",
-    "zdm1", "zdp2", "zfm3", "zfp3", "zdp1", "yfp3", "g2", "yfm3", "zl2", "zdp3", "zdm3", "zl1", "wr1", "Pa0",
-    "zl3", "PaA", "wr2", "PbA", "IA1", "IA3", "Pa3", "Pb0", "Pb3", "D20", "IA2", "D31", "IB2", "D10", "IA0",
-    "E20", "D21", "D11", "E31", "D30", "E21", "D00", "IB1", "E10", "IB3", "E11", "sent", "E30", "R1", "Zc0",
-    "E00", "Zd0", "R2", "D01", "V3p", "E01", "V3m", "S0", "Zd1", "Zd2", "Zc1", "ZL0", "IB0", "Zc2", "R3",
-    "Vm", "Zd3", "ZL1", "Vp", "ZL2", "Zc3", "R0", "RF", "ZL3",
+    "mask", "wa2", "zfp0", "yfp0", "yfm0", "xa2", "zfm0", "xb1", "wb2", "wa1", "w2s", "g13", "xb2", "zdp0",
+    "xa1", "wb1", "zfm2", "zfp2", "wa3", "zdm0", "zdp2", "xb3", "zl0", "yfm1", "xy1", "wb3", "xa3", "yfp2",
+    "zfp1", "xy3", "zdm2", "zfm1", "zfp3", "zfm3", "zl2", "zdp1", "zdm1", "zdm3", "yfm3", "zdp3", "g2",
+    "yfp3", "wr1", "zl1", "Pa0", "zl3", "PaA", "wr2", "PbA", "IA1", "IA3", "Pa3", "Pb0", "Pb3", "D20", "IB2",
+    "IA2", "IA0", "D21", "E20", "D10", "IB3", "IB1", "D30", "E21", "D31", "D11", "E10", "R1", "E30", "D00",
+    "D01", "E31", "E11", "Zc1", "R2", "Zd0", "Zc0", "Zc2", "E00", "Zd1", "Zd2", "Zd3", "IB0", "sent", "E01",
+    "S0", "Zc3", "R3", "ZL0", "Vp", "Vm", "ZL1", "ZL2", "R0", "ZL3", "RF",
 )
 
 def kernel(
     x_ref, g_ref, w_ref, wid_ref, dx_ref, dw_ref,
-    xb, wb, gb, gin, wid, acc, hid, sd, qb, vp, vm, vp3, vm3, ap, am, rb, xr, own, out,
+    xb, wb, gb, gin, wid, acc, hid, sd, qb, vp, vm, ap, am, rb, xr, own, out,
     dwp, dwr, dws, zvp, zvm, zap, zam, tot, ssem, rsem, lsem,
 ):
     dp, tensor = lax.axis_index("dp"), lax.axis_index("tensor")
@@ -103,10 +103,6 @@
     )
     own_g = pltpu.make_async_copy(g_ref, gin, lsem.at[0])
     own_wid = pltpu.make_async_copy(wid_ref, wid, lsem.at[3])
-    own_wid.start()
-    own_g.start()
-    own_x.start()
-    own_w.start()
     put_g = pltpu.make_async_copy(
         gin.at[half_of(c), sub_block(0)], gb.at[place(0), own_cols], lsem.at[0]
     )
@@ -120,6 +116,10 @@
     barrier = pltpu.get_barrier_semaphore()
     for to in partners:
         pl.semaphore_signal(barrier, inc=1, device_id=device(**to), device_id_type=MESH)
+    own_wid.start()
+    own_g.start()
+    own_x.start()
+    own_w.start()
     pl.semaphore_wait(barrier, len(partners))
 
     tasks = {}
@@ -182,9 +182,10 @@
         ref = xb.at[chunk(1, other), place(j)]
         send(f"yfm{j}", ref, ref, dy=3)
 
-    def w_send(step):
-        dst = wb.at[weight_rows(0, 0), own_cols]
-        send(f"w{step}", w_ref.at[:, sub_block(step)], dst, dx=step)
+    def w_send(step, half):
+        src = w_ref.at[pl.ds(half * 96, 96), sub_block(step)]
+        dst = wb.at[weight_half(0, 0, half), own_cols]
+        send(f"w{step}{'ab'[half]}", src, dst, dx=step)
 
     def z_send(j, name, half):
         to = 1 if name == "zp" else 3
@@ -194,13 +195,12 @@
         dst = wb.at[weight_half(4 - to, STEP[j], half), own_cols]
         send(f"{name}{j}{'ab'[half]}", src, dst, dz=to)
 
-    def w_arrive(j):
-        arrived(f"w{FROM[j]}")
-        z_send(j, "zp", 0)
-        z_send(j, "zm", 1)
-        z_send(j, "zp", 1)
-        z_send(j, "zm", 0)
-        w_pair(f"ws{j}", 0, j)
+    def w_arrive(j, half):
+        arrived(f"w{FROM[j]}{'ab'[half]}")
+        for name in ("zm", "zp") if half else ("zp", "zm"):
+            z_send(j, name, half)
+        ref = wb.at[weight_half(0, STEP[j], half), own_cols]
+        send(f"ws{'ab'[half]}{j}", ref, ref, dc=1)
 
     def w_pair(name, dz, j):
         dst = wb.at[weight_rows(dz, STEP[j]), own_cols]
@@ -231,13 +231,15 @@
 
     @task("w2s")
     def w_across():
-        w_send(2)
+        w_send(2, 0)
+        w_send(2, 1)
 
     @task("wr1")
     def weights_near():
         own_w.wait()
         for j in range(4):
-            arrived(f"ws{j}", f"d1{j}", f"d3{j}")
+            arrived(f"d1{j}", f"d3{j}")
+            arrived(*((f"wsa{j}", f"wsb{j}") if j else ("ws0",)))
 
     @task("wr2")
     def weights_across():
@@ -280,7 +282,8 @@
         if j:
             task(f"xa{j}", j, "s")(x_arrive)
             task(f"xb{j}", j, "o")(x_arrive)
-            task(f"wa{j}", j)(w_arrive)
+            task(f"wa{j}", j, 0)(w_arrive)
+            task(f"wb{j}", j, 1)(w_arrive)
         task(f"yfp{j}", j)(y_forward_up)
         task(f"yfm{j}", j)(y_forward_down)
         task(f"zfp{j}", j)(z_forward_up)
@@ -332,7 +335,6 @@
 
     first, second = pl.ds(0, 128), pl.ds(128, 128)
     upper, lower = pl.ds(0, 64), pl.ds(64, 64)
-    upper3, lower3 = pl.ds(128, 64), pl.ds(192, 64)
 
     def input_part(b, d):
         dz = lax.rem(y + d - z + 4, 4)
@@ -345,8 +347,7 @@
             send("q1", sd.at[0, 2, first], qb.at[0], dx=1)
             send("q3", sd.at[0, 2, second], qb.at[1], dx=3)
         elif d == 2:
-            send("vp3", sd.at[1, 2, upper3], vp3, dy=1)
-            send("vm3", sd.at[1, 2, lower3], vm3, dy=3)
+            send("q2", sd.at[1, 2, second], qb.at[2], dx=2)
         elif d == 1 and b == 0:
             send("a11", sd.at[0, 1, first], ap.at[0], dy=1)
             send("a12", sd.at[0, 1, second], ap.at[1], dy=1)
@@ -354,10 +355,10 @@
             send("a31", sd.at[0, 3, first], am.at[0], dy=3)
             send("a32", sd.at[0, 3, second], am.at[1], dy=3)
         elif d == 1:
-            send("a13l", sd.at[1, 1, lower3], ap.at[3, lower], dy=1)
+            send("a13", sd.at[1, 1, second], ap.at[3], dy=1)
             send("a10l", sd.at[1, 1, lower], ap.at[2, lower], dy=1)
         elif d == 3:
-            send("a33t", sd.at[1, 3, upper3], am.at[3, upper], dy=3)
+            send("a33", sd.at[1, 3, second], am.at[3], dy=3)
             send("a30t", sd.at[1, 3, upper], am.at[2, upper], dy=3)
 
     for b in range(2):
@@ -366,32 +367,29 @@
 
     @task("S0")
     def across_total():
-        arrived("q1", "q3")
+        arrived("q1", "q3", "q2")
         total = sd[1, 2, first].astype(F32)
-        for slot in range(2):
+        for slot in range(3):
             total = total + qb[slot].astype(F32)
         sd[1, 2, first] = total.astype(BF16)
         send("vp", sd.at[1, 2, upper], vp, dy=1)
         send("vm", sd.at[1, 2, lower], vm, dy=3)
 
-    def via_up(name, came, rows, to, at):
-        arrived(name)
-        sd[1, 1, rows] = (sd[1, 1, rows].astype(F32) + came[...].astype(F32)).astype(BF16)
-        send(to, sd.at[1, 1, rows], ap.at[at, upper], dy=1)
-
-    def via_down(name, came, rows, to, at):
-        arrived(name)
-        sd[1, 3, rows] = (sd[1, 3, rows].astype(F32) + came[...].astype(F32)).astype(BF16)
-        send(to, sd.at[1, 3, rows], am.at[at, lower], dy=3)
-
-    task("Vp", "vp", vp, upper, "a10t", 2)(via_up)
-    task("Vm", "vm", vm, lower, "a30l", 2)(via_down)
-    task("V3p", "vp3", vp3, upper3, "a13t", 3)(via_up)
-    task("V3m", "vm3", vm3, lower3, "a33l", 3)(via_down)
+    @task("Vp")
+    def via_up():
+        arrived("vp")
+        sd[1, 1, upper] = (sd[1, 1, upper].astype(F32) + vp[...].astype(F32)).astype(BF16)
+        send("a10t", sd.at[1, 1, upper], ap.at[2, upper], dy=1)
+
+    @task("Vm")
+    def via_down():
+        arrived("vm")
+        sd[1, 3, lower] = (sd[1, 3, lower].astype(F32) + vm[...].astype(F32)).astype(BF16)
+        send("a30l", sd.at[1, 3, lower], am.at[2, lower], dy=3)
 
     def input_total(j):
-        if j in (0, 3):
-            arrived(f"a1{j}l", f"a1{j}t", f"a3{j}t", f"a3{j}l")
+        if j == 0:
+            arrived("a10l", "a10t", "a30t", "a30l")
         else:
             arrived(f"a1{j}", f"a3{j}")
         at, rows = PLACE[j], (first, second)[PLACE[j] % 2]
@@ -505,10 +503,12 @@
         for name in left:
             sites[name].wait_send()
 
+    w_send(1, 0)
+    w_send(3, 1)
     x_send(1, "s")
     x_send(3, "o")
-    w_send(1)
-    w_send(3)
+    w_send(1, 1)
+    w_send(3, 0)
     x_send(1, "o")
     x_send(3, "s")
     y_send(0, "yp", "s")
@@ -571,9 +571,7 @@
             pltpu.VMEM((4 * HALF, 2 * COLS), F32),
             buffer(4 * HALF, 2 * COLS),
             buffer(2, 4, 2 * HALF, 2 * COLS),
-            buffer(2, HALF, 2 * COLS),
-            buffer(64, 2 * COLS),
-            buffer(64, 2 * COLS),
+            buffer(3, HALF, 2 * COLS),
             buffer(64, 2 * COLS),
             buffer(64, 2 * COLS),
             buffer(4, HALF, 2 * COLS),

time: 71.4 us -> 68.3 us (0.957)
  Pallas kernels: 70.6 us -> 67.5 us
    pallas_call x1, Pallas kernels: 68.7 us -> 65.6 us  [shards(): pl.pallas_call(kernel, out_shape=results, in_specs=[any_space] * 4, out_s...]
where the time goes in v5:
time: 68.3 us; the launch traced here: 68.1 us
  Pallas kernels  67.5 us (99%)
    pallas_call x1, Pallas kernels, shards(): pl.pallas_call(kernel, out_shape=results, in_specs=[any_space] * 4, out_s...  65.6 us
    pallas_call x1, Pallas kernels, shards(): pl.pallas_call(hand_on, out_shape=results, in_specs=[any_space] * 2, out_...  1.89 us

profile of v5, /device:TPU:1, one launch (start us, length us, event | category | flops | bytes accessed | tf_op | source)
XLA Modules:
  0.0 68.1 jit_solution(10275064699393943663)
XLA Ops:
  0.6 65.6 %elastic_up_backward.1 = (bf16[256,384]{1,0:T(8,128)(2,1)}, bf16[192,1536]{1,0:T(8,128)(2,1)}) custom-call(bf16[256,384]{1,0:T(8,128)(2,1)} %x_ref.1, bf16[256,1536]{1,0:T(8,128)(2,1)} %g_ref.1, bf16[192,1536]{1,0:T(8,128)(2,1)} %w_ref.1, s32[2,128]{1,0:T(2,128)} %bitcast.1), custom_call_target="tpu_custom_call" | custom-call | flops 7247757312 | bytes 4194304 | tf_op jit(solution)/shard_map/elastic_up_backward/pallas_call | solution.py:560
  66.3 1.9 %hand_on.1 = (bf16[256,384]{1,0:T(8,128)(2,1)}, bf16[192,1536]{1,0:T(8,128)(2,1)}) custom-call(bf16[256,384]{1,0:T(8,128)(2,1)} %get-tuple-element.4.a_ref, bf16[192,1536]{1,0:T(8,128)(2,1)} %get-tuple-element.5.b_ref), custom_call_target="tpu_custom_call" | custom-call | tf_op jit(solution)/shard_map/hand_on/pallas_call | solution.py:603

commit v6 on v5

--- a/solution.py
+++ b/solution.py
@@ -14,7 +14,7 @@
 COLS = 384
 HID = 1536
 SCALE = 1.0 / 64.0
-N_SEM = 176
+N_SEM = 208
 
 STEP = (0, 1, 3, 2)
 FROM = (0, 3, 1, 2)
@@ -23,18 +23,19 @@
 SUB = (2, 1, 3, 0)
 
 ORDER = (
-    "mask", "wa2", "zfp0", "yfp0", "yfm0", "xa2", "zfm0", "xb1", "wb2", "wa1", "w2s", "g13", "xb2", "zdp0",
-    "xa1", "wb1", "zfm2", "zfp2", "wa3", "zdm0", "zdp2", "xb3", "zl0", "yfm1", "xy1", "wb3", "xa3", "yfp2",
-    "zfp1", "xy3", "zdm2", "zfm1", "zfp3", "zfm3", "zl2", "zdp1", "zdm1", "zdm3", "yfm3", "zdp3", "g2",
-    "yfp3", "wr1", "zl1", "Pa0", "zl3", "PaA", "wr2", "PbA", "IA1", "IA3", "Pa3", "Pb0", "Pb3", "D20", "IB2",
-    "IA2", "IA0", "D21", "E20", "D10", "IB3", "IB1", "D30", "E21", "D31", "D11", "E10", "R1", "E30", "D00",
-    "D01", "E31", "E11", "Zc1", "R2", "Zd0", "Zc0", "Zc2", "E00", "Zd1", "Zd2", "Zd3", "IB0", "sent", "E01",
-    "S0", "Zc3", "R3", "ZL0", "Vp", "Vm", "ZL1", "ZL2", "R0", "ZL3", "RF",
+    "wb1", "zfp0", "yfm0", "zfm0", "yfp0", "wa2", "xa2", "zdm0", "xb1", "w2s", "wb2", "xb2", "zfm1", "wa1",
+    "xa3", "zfp2", "zdp0", "mask", "g13", "xa1", "xb3", "xy1", "wa3", "wb3", "yfm1", "yfp2", "zl0", "zdm1",
+    "xy3", "zfp1", "zfm2", "yfp3", "zfp3", "g2", "zfm3", "zdm2", "zdp3", "zdp1", "zdp2", "zdm3", "yfm3",
+    "zl1", "wr1", "zl2", "Pa0", "zl3", "PaA", "wr2", "PbA", "IA3", "IA1", "Pb3", "Pb0", "D21", "D20", "IB2",
+    "sent", "D10", "D30", "E21", "E20", "Zv0", "Zv1", "IA2", "D31", "D11", "E30", "IB3", "IA0", "Zv2", "E10",
+    "Ql", "E31", "Qu", "R2s", "IB1", "E11", "Zd1", "R1s", "Zc0", "IB0", "D01", "R1o", "R2o", "Zd0", "Zc2",
+    "Zc1", "R3s", "S0", "Zd2", "Zv3", "D00", "E01", "R3o", "E00", "ZL0", "Zd3", "Vm", "Vp", "ZL1", "ZL2",
+    "Zc3", "RF", "ZL3",
 )
 
 def kernel(
     x_ref, g_ref, w_ref, wid_ref, dx_ref, dw_ref,
-    xb, wb, gb, gin, wid, acc, hid, sd, qb, vp, vm, ap, am, rb, xr, own, out,
+    xb, wb, gb, gin, wid, acc, hid, sd, qb, qv, vp, vm, ap, am, ap0, am0, rb, xr, own, out,
     dwp, dwr, dws, zvp, zvm, zap, zam, tot, ssem, rsem, lsem,
 ):
     dp, tensor = lax.axis_index("dp"), lax.axis_index("tensor")
@@ -94,6 +95,8 @@
         return pl.ds(pl.multiple_of(ring(x, step) * COLS, COLS), COLS)
 
     own_cols = pl.ds(pl.multiple_of(c * COLS, COLS), COLS)
+    other_cols = pl.ds(pl.multiple_of(other * COLS, COLS), COLS)
+    both = (("s", own_cols, 0), ("o", other_cols, 1))
 
     own_w = pltpu.make_async_copy(
         w_ref.at[:, sub_block(0)], wb.at[weight_rows(0, 0), own_cols], lsem.at[2]
@@ -298,7 +301,7 @@
     def batch(places):
         return pl.ds(PLACE[places[0]] * HALF, HALF * len(places))
 
-    def hidden_near(*places):
+    def tokens_ready(*places):
         for j in places:
             arrived(f"yp{j}o", f"ym{j}s")
             if j == 1:
@@ -312,6 +315,9 @@
             if j == 0:
                 own_x.wait()
                 arrived("xs")
+
+    def hidden_near(*places):
+        tokens_ready(*places)
         rows = batch(places)
         part = jnp.concatenate(features(0, rows) + features(1, rows) + features(3, rows), axis=1)
         acc[rows, :] = jnp.dot(part, wb[pl.ds(0, 2304), :], preferred_element_type=F32)
@@ -324,17 +330,24 @@
             else:
                 arrived(f"g{FROM[j]}s", f"g{FROM[j]}o")
         rows = batch(places)
-        part = jnp.concatenate(features(2, rows), axis=1)
-        preact = acc[rows, :] + jnp.dot(part, wb[pl.ds(2304, 768), :], preferred_element_type=F32)
+        if places == (3,):
+            tokens_ready(3)
+            part = jnp.concatenate(sum((features(d, rows) for d in (0, 1, 3, 2)), []), axis=1)
+            preact = jnp.dot(part, wb[...], preferred_element_type=F32)
+        else:
+            part = jnp.concatenate(features(2, rows), axis=1)
+            preact = acc[rows, :] + jnp.dot(part, wb[pl.ds(2304, 768), :], preferred_element_type=F32)
         slope = 2.0 * jnp.maximum(preact, 0.0)
         hid[rows, :] = (gb[rows, :].astype(F32) * slope).astype(BF16)
 
     for name, places in (("A", (1, 2)), ("0", (0,)), ("3", (3,))):
-        task("Pa" + name, *places)(hidden_near)
+        if name != "3":
+            task("Pa" + name, *places)(hidden_near)
         task("Pb" + name, *places)(hidden_last)
 
     first, second = pl.ds(0, 128), pl.ds(128, 128)
     upper, lower = pl.ds(0, 64), pl.ds(64, 64)
+    upper2, lower2 = pl.ds(128, 64), pl.ds(192, 64)
 
     def input_part(b, d):
         dz = lax.rem(y + d - z + 4, 4)
@@ -344,33 +357,48 @@
             hid[pl.ds(b * 256, 256), :], wb[rows, :], (((1,), (1,)), ((), ())), preferred_element_type=F32
         ).astype(BF16)
         if d == 2 and b == 0:
-            send("q1", sd.at[0, 2, first], qb.at[0], dx=1)
-            send("q3", sd.at[0, 2, second], qb.at[1], dx=3)
+            send("q1l", sd.at[0, 2, lower], qb.at[0, lower], dx=1)
+            send("q3u", sd.at[0, 2, upper2], qb.at[1, upper], dx=3)
         elif d == 2:
-            send("q2", sd.at[1, 2, second], qb.at[2], dx=2)
-        elif d == 1 and b == 0:
-            send("a11", sd.at[0, 1, first], ap.at[0], dy=1)
-            send("a12", sd.at[0, 1, second], ap.at[1], dy=1)
-        elif d == 3 and b == 0:
-            send("a31", sd.at[0, 3, first], am.at[0], dy=3)
-            send("a32", sd.at[0, 3, second], am.at[1], dy=3)
-        elif d == 1:
-            send("a13", sd.at[1, 1, second], ap.at[3], dy=1)
-            send("a10l", sd.at[1, 1, lower], ap.at[2, lower], dy=1)
-        elif d == 3:
-            send("a33", sd.at[1, 3, second], am.at[3], dy=3)
-            send("a30t", sd.at[1, 3, upper], am.at[2, upper], dy=3)
+            send("q2a", sd.at[1, 2, upper2], qv.at[0], dx=1)
+            send("q2b", sd.at[1, 2, lower2], qv.at[1], dx=3)
+        elif d == 0 and b == 1:
+            own[c] = sd[1, 0, first, own_cols]
+            send("xro", sd.at[1, 0, first, other_cols], own.at[c], dc=1)
+        elif d != 0:
+            got, dy = (ap, 1) if d == 1 else (am, 3)
+            for kind, cols, _ in both:
+                for j in (1, 2) if b == 0 else (3,):
+                    rows = second if PLACE[j] % 2 else first
+                    send(f"a{d}{j}{kind}", sd.at[b, d, rows, cols], got.at[PLACE[j], :, cols], dy=dy)
+            if b == 1:
+                own_send("a10l" if d == 1 else "a30t", d, lower if d == 1 else upper)
+
+    def own_send(name, d, rows):
+        got, dy = (ap0, 1) if d == 1 else (am0, 3)
+        for kind, cols, dc in both:
+            send(name + kind, sd.at[1, d, rows, cols], got.at[c, rows], dy=dy, dc=dc)
 
     for b in range(2):
         for d in range(4):
             task(f"I{'AB'[b]}{d}", b, d)(input_part)
 
+    @task("Qu")
+    def across_up():
+        arrived("q2a")
+        sd[0, 2, upper] = (sd[0, 2, upper].astype(F32) + qv[0].astype(F32)).astype(BF16)
+        send("q1u", sd.at[0, 2, upper], qb.at[0, upper], dx=1)
+
+    @task("Ql")
+    def across_down():
+        arrived("q2b")
+        sd[0, 2, lower2] = (sd[0, 2, lower2].astype(F32) + qv[1].astype(F32)).astype(BF16)
+        send("q3l", sd.at[0, 2, lower2], qb.at[1, lower], dx=3)
+
     @task("S0")
     def across_total():
-        arrived("q1", "q3", "q2")
-        total = sd[1, 2, first].astype(F32)
-        for slot in range(3):
-            total = total + qb[slot].astype(F32)
+        arrived("q1l", "q1u", "q3u", "q3l")
+        total = sd[1, 2, first].astype(F32) + qb[0].astype(F32) + qb[1].astype(F32)
         sd[1, 2, first] = total.astype(BF16)
         send("vp", sd.at[1, 2, upper], vp, dy=1)
         send("vm", sd.at[1, 2, lower], vm, dy=3)
@@ -379,40 +407,34 @@
     def via_up():
         arrived("vp")
         sd[1, 1, upper] = (sd[1, 1, upper].astype(F32) + vp[...].astype(F32)).astype(BF16)
-        send("a10t", sd.at[1, 1, upper], ap.at[2, upper], dy=1)
+        own_send("a10t", 1, upper)
 
     @task("Vm")
     def via_down():
         arrived("vm")
         sd[1, 3, lower] = (sd[1, 3, lower].astype(F32) + vm[...].astype(F32)).astype(BF16)
-        send("a30l", sd.at[1, 3, lower], am.at[2, lower], dy=3)
-
-    def input_total(j):
-        if j == 0:
-            arrived("a10l", "a10t", "a30t", "a30l")
-        else:
-            arrived(f"a1{j}", f"a3{j}")
+        own_send("a30l", 3, lower)
+
+    def input_total(j, kind, cols, dc):
+        arrived(f"a1{j}{kind}", f"a3{j}{kind}")
         at, rows = PLACE[j], (first, second)[PLACE[j] % 2]
-        total = sd[at // 2, 0, rows].astype(F32) + ap[at].astype(F32) + am[at].astype(F32)
-        total = total.astype(BF16)
-        rb[at, 0] = total[:, :COLS]
-        rb[at, 1] = total[:, COLS:]
-        if j == 0:
-            own[c] = rb[at, c]
-            send("xro", rb.at[at, other], own.at[c], dc=1)
-        else:
-            step = STEP[j]
-            send(f"xr{step}s", rb.at[at, c], xr.at[step - 1, c], dx=step)
-            send(f"xr{step}o", rb.at[at, other], xr.at[step - 1, c], dx=step, dc=1)
-
-    for j in range(4):
-        task(f"R{j}", j)(input_total)
+        total = (
+            sd[at // 2, 0, rows, cols].astype(F32) + ap[at, :, cols].astype(F32) + am[at, :, cols].astype(F32)
+        )
+        rb[at, dc] = total.astype(BF16)
+        send(f"xr{STEP[j]}{kind}", rb.at[at, dc], xr.at[STEP[j] - 1, c], dx=STEP[j], dc=dc)
+
+    for j in range(1, 4):
+        for kind, cols, dc in both:
+            task(f"R{j}{kind}", j, kind, cols, dc)(input_total)
 
     @task("RF")
     def input_final():
         arrived("xr1s", "xr1o", "xr3s", "xr3o", "xr2s", "xr2o", "xro")
+        for name in ("a10l", "a10t", "a30t", "a30l"):
+            arrived(name + "s", name + "o")
         for half in range(2):
-            total = own[half].astype(F32)
+            total = own[half].astype(F32) + ap0[half].astype(F32) + am0[half].astype(F32)
             for slot in range(3):
                 total = total + xr[slot, half].astype(F32)
             out[pl.ds(half * HALF, HALF), :] = total.astype(BF16)
@@ -435,9 +457,6 @@
             rows = pl.ds(pl.multiple_of(at * 96, 96), 96)
             dws[d, 0, rows] = total[p * ROWS : p * ROWS + 96]
             dws[d, 1, rows] = total[p * ROWS + 96 : p * ROWS + ROWS]
-            if d == 2:
-                via_copy("zvp", at, rows).start()
-                via_copy("zvm", at, rows).start()
 
     for d in range(4):
         for h in range(2):
@@ -447,23 +466,10 @@
     def sub_rows(q):
         return pl.ds(q * 96, 96)
 
-    via_slots = {}
-
-    def via_copy(name, at, rows):
-        up = name == "zvp"
-        return pltpu.make_async_remote_copy(
-            src_ref=dws.at[2, 0 if up else 1, rows],
-            dst_ref=(zvp if up else zvm).at[rows],
-            send_sem=ssem.at[via_slots[name] + at],
-            recv_sem=rsem.at[via_slots[name] + at],
-            device_id=device(dz=1 if up else 3),
-            device_id_type=MESH,
-        )
-
-    for name in ("zvp", "zvm"):
-        via_slots[name] = len(sites)
-        for q in range(4):
-            sites[f"{name}{q}"] = via_copy(name, q, sub_rows(q))
+    def weight_first(q):
+        rows = sub_rows(q)
+        send(f"zvp{q}", dws.at[2, 0, rows], zvp.at[rows], dz=1)
+        send(f"zvm{q}", dws.at[2, 1, rows], zvm.at[rows], dz=3)
 
     def weight_direct(q):
         rows = sub_rows(q)
@@ -492,6 +498,7 @@
             put_w.start()
 
     for q in range(4):
+        task(f"Zv{q}", q)(weight_first)
         task(f"Zd{q}", q)(weight_direct)
         task(f"Zc{q}", q)(weight_via)
         task(f"ZL{q}", q)(weight_last)
@@ -522,8 +529,8 @@
     w_pair("ws0", 0, 0)
     send("xs", x_ref.at[half_of(other)], xb.at[chunk(0, c), place(0)], dc=1)
     for name in ORDER:
-        if name == "PbA":
-            left.extend(n for n in sites if n[:2] != "zv")
+        if not left and name[0] in "ID":
+            left.extend(sites)
         tasks[name]()
     for name, copy in sites.items():
         if name not in left:
@@ -571,11 +578,14 @@
             pltpu.VMEM((4 * HALF, 2 * COLS), F32),
             buffer(4 * HALF, 2 * COLS),
             buffer(2, 4, 2 * HALF, 2 * COLS),
-            buffer(3, HALF, 2 * COLS),
+            buffer(2, HALF, 2 * COLS),
+            buffer(2, 64, 2 * COLS),
             buffer(64, 2 * COLS),
             buffer(64, 2 * COLS),
             buffer(4, HALF, 2 * COLS),
             buffer(4, HALF, 2 * COLS),
+            buffer(2, HALF, COLS),
+            buffer(2, HALF, COLS),
             buffer(4, 2, HALF, COLS),
             buffer(3, 2, HALF, COLS),
             buffer(2, HALF, COLS),

time: 68.3 us -> 68.4 us (level)
  no operation moved by 1% of the time
where the time goes in v6:
time: 68.4 us; the launch traced here: 68.2 us
  Pallas kernels  67.6 us (99%)
    pallas_call x1, Pallas kernels, shards(): pl.pallas_call(kernel, out_shape=results, in_specs=[any_space] * 4, out_s...  65.7 us
    pallas_call x1, Pallas kernels, shards(): pl.pallas_call(hand_on, out_shape=results, in_specs=[any_space] * 2, out_...  1.89 us

profile of v6, /device:TPU:1, one launch (start us, length us, event | category | flops | bytes accessed | tf_op | source)
XLA Modules:
  0.0 68.2 jit_solution(80052908221617044)
XLA Ops:
  0.6 65.7 %elastic_up_backward.1 = (bf16[256,384]{1,0:T(8,128)(2,1)}, bf16[192,1536]{1,0:T(8,128)(2,1)}) custom-call(bf16[256,384]{1,0:T(8,128)(2,1)} %x_ref.1, bf16[256,1536]{1,0:T(8,128)(2,1)} %g_ref.1, bf16[192,1536]{1,0:T(8,128)(2,1)} %w_ref.1, s32[2,128]{1,0:T(2,128)} %bitcast.1), custom_call_target="tpu_custom_call" | custom-call | flops 7247757312 | bytes 4194304 | tf_op jit(solution)/shard_map/elastic_up_backward/pallas_call | solution.py:567
  66.3 1.9 %hand_on.1 = (bf16[256,384]{1,0:T(8,128)(2,1)}, bf16[192,1536]{1,0:T(8,128)(2,1)}) custom-call(bf16[256,384]{1,0:T(8,128)(2,1)} %get-tuple-element.4.a_ref, bf16[192,1536]{1,0:T(8,128)(2,1)} %get-tuple-element.5.b_ref), custom_call_target="tpu_custom_call" | custom-call | tf_op jit(solution)/shard_map/hand_on/pallas_call | solution.py:613

commit v7 on v5

--- a/solution.py
+++ b/solution.py
@@ -26,7 +26,7 @@
     "mask", "wa2", "zfp0", "yfp0", "yfm0", "xa2", "zfm0", "xb1", "wb2", "wa1", "w2s", "g13", "xb2", "zdp0",
     "xa1", "wb1", "zfm2", "zfp2", "wa3", "zdm0", "zdp2", "xb3", "zl0", "yfm1", "xy1", "wb3", "xa3", "yfp2",
     "zfp1", "xy3", "zdm2", "zfm1", "zfp3", "zfm3", "zl2", "zdp1", "zdm1", "zdm3", "yfm3", "zdp3", "g2",
-    "yfp3", "wr1", "zl1", "Pa0", "zl3", "PaA", "wr2", "PbA", "IA1", "IA3", "Pa3", "Pb0", "Pb3", "D20", "IB2",
+    "yfp3", "wr1", "zl1", "Pa0", "zl3", "PaA", "wr2", "PbA", "IA1", "IA3", "Pb0", "Pb3", "D20", "IB2",
     "IA2", "IA0", "D21", "E20", "D10", "IB3", "IB1", "D30", "E21", "D31", "D11", "E10", "R1", "E30", "D00",
     "D01", "E31", "E11", "Zc1", "R2", "Zd0", "Zc0", "Zc2", "E00", "Zd1", "Zd2", "Zd3", "IB0", "sent", "E01",
     "S0", "Zc3", "R3", "ZL0", "Vp", "Vm", "ZL1", "ZL2", "R0", "ZL3", "RF",
@@ -298,7 +298,7 @@
     def batch(places):
         return pl.ds(PLACE[places[0]] * HALF, HALF * len(places))
 
-    def hidden_near(*places):
+    def tokens_ready(*places):
         for j in places:
             arrived(f"yp{j}o", f"ym{j}s")
             if j == 1:
@@ -312,6 +312,9 @@
             if j == 0:
                 own_x.wait()
                 arrived("xs")
+
+    def hidden_near(*places):
+        tokens_ready(*places)
         rows = batch(places)
         part = jnp.concatenate(features(0, rows) + features(1, rows) + features(3, rows), axis=1)
         acc[rows, :] = jnp.dot(part, wb[pl.ds(0, 2304), :], preferred_element_type=F32)
@@ -324,13 +327,19 @@
             else:
                 arrived(f"g{FROM[j]}s", f"g{FROM[j]}o")
         rows = batch(places)
-        part = jnp.concatenate(features(2, rows), axis=1)
-        preact = acc[rows, :] + jnp.dot(part, wb[pl.ds(2304, 768), :], preferred_element_type=F32)
+        if places == (3,):
+            tokens_ready(3)
+            part = jnp.concatenate(sum((features(d, rows) for d in (0, 1, 3, 2)), []), axis=1)
+            preact = jnp.dot(part, wb[...], preferred_element_type=F32)
+        else:
+            part = jnp.concatenate(features(2, rows), axis=1)
+            preact = acc[rows, :] + jnp.dot(part, wb[pl.ds(2304, 768), :], preferred_element_type=F32)
         slope = 2.0 * jnp.maximum(preact, 0.0)
         hid[rows, :] = (gb[rows, :].astype(F32) * slope).astype(BF16)
 
     for name, places in (("A", (1, 2)), ("0", (0,)), ("3", (3,))):
-        task("Pa" + name, *places)(hidden_near)
+        if name != "3":
+            task("Pa" + name, *places)(hidden_near)
         task("Pb" + name, *places)(hidden_last)
 
     first, second = pl.ds(0, 128), pl.ds(128, 128)

time: 68.3 us -> 68.2 us (level)
  no operation moved by 1% of the time
where the time goes in v7:
time: 68.2 us; the launch traced here: 68 us
  Pallas kernels  67.4 us (99%)
    pallas_call x1, Pallas kernels, shards(): pl.pallas_call(kernel, out_shape=results, in_specs=[any_space] * 4, out_s...  65.5 us
    pallas_call x1, Pallas kernels, shards(): pl.pallas_call(hand_on, out_shape=results, in_specs=[any_space] * 2, out_...  1.89 us

profile of v7, /device:TPU:1, one launch (start us, length us, event | category | flops | bytes accessed | tf_op | source)
XLA Modules:
  0.0 68.0 jit_solution(7350985978019534762)
XLA Ops:
  0.6 65.5 %elastic_up_backward.1 = (bf16[256,384]{1,0:T(8,128)(2,1)}, bf16[192,1536]{1,0:T(8,128)(2,1)}) custom-call(bf16[256,384]{1,0:T(8,128)(2,1)} %x_ref.1, bf16[256,1536]{1,0:T(8,128)(2,1)} %g_ref.1, bf16[192,1536]{1,0:T(8,128)(2,1)} %w_ref.1, s32[2,128]{1,0:T(2,128)} %bitcast.1), custom_call_target="tpu_custom_call" | custom-call | flops 7247757312 | bytes 4194304 | tf_op jit(solution)/shard_map/elastic_up_backward/pallas_call | solution.py:569
  66.1 1.9 %hand_on.1 = (bf16[256,384]{1,0:T(8,128)(2,1)}, bf16[192,1536]{1,0:T(8,128)(2,1)}) custom-call(bf16[256,384]{1,0:T(8,128)(2,1)} %get-tuple-element.4.a_ref, bf16[192,1536]{1,0:T(8,128)(2,1)} %get-tuple-element.5.b_ref), custom_call_target="tpu_custom_call" | custom-call | tf_op jit(solution)/shard_map/hand_on/pallas_call | solution.py:612

commit v8 on v7

--- a/solution.py
+++ b/solution.py
@@ -26,10 +26,10 @@
     "mask", "wa2", "zfp0", "yfp0", "yfm0", "xa2", "zfm0", "xb1", "wb2", "wa1", "w2s", "g13", "xb2", "zdp0",
     "xa1", "wb1", "zfm2", "zfp2", "wa3", "zdm0", "zdp2", "xb3", "zl0", "yfm1", "xy1", "wb3", "xa3", "yfp2",
     "zfp1", "xy3", "zdm2", "zfm1", "zfp3", "zfm3", "zl2", "zdp1", "zdm1", "zdm3", "yfm3", "zdp3", "g2",
-    "yfp3", "wr1", "zl1", "Pa0", "zl3", "PaA", "wr2", "PbA", "IA1", "IA3", "Pb0", "Pb3", "D20", "IB2",
-    "IA2", "IA0", "D21", "E20", "D10", "IB3", "IB1", "D30", "E21", "D31", "D11", "E10", "R1", "E30", "D00",
-    "D01", "E31", "E11", "Zc1", "R2", "Zd0", "Zc0", "Zc2", "E00", "Zd1", "Zd2", "Zd3", "IB0", "sent", "E01",
-    "S0", "Zc3", "R3", "ZL0", "Vp", "Vm", "ZL1", "ZL2", "R0", "ZL3", "RF",
+    "yfp3", "wr1", "zl1", "Pa0", "zl3", "PaA", "wr2", "PbA", "IA1", "IA3", "IA2", "Pb0", "Pb3", "D20", "IB2",
+    "IA0", "D21", "E20", "D10", "IB3", "IB1", "D30", "E21", "D31", "D11", "E10", "R1", "E30", "D00", "D01",
+    "E31", "E11", "Zc1", "R2", "Zd0", "Zc0", "Zc2", "E00", "sent", "Zd1", "Zd2", "Zd3", "IB0", "E01", "S0",
+    "Zc3", "R3", "ZL0", "Vp", "Vm", "ZL1", "ZL2", "R0", "ZL3", "RF",
 )
 
 def kernel(

time: 68.2 us -> 68.5 us (level)
  no operation moved by 1% of the time
where the time goes in v8:
time: 68.5 us; the launch traced here: 68.4 us
  Pallas kernels  67.7 us (99%)
    pallas_call x1, Pallas kernels, shards(): pl.pallas_call(kernel, out_shape=results, in_specs=[any_space] * 4, out_s...  65.8 us
    pallas_call x1, Pallas kernels, shards(): pl.pallas_call(hand_on, out_shape=results, in_specs=[any_space] * 2, out_...  1.89 us

profile of v8, /device:TPU:1, one launch (start us, length us, event | category | flops | bytes accessed | tf_op | source)
XLA Modules:
  0.0 68.4 jit_solution(2834528021370790183)
XLA Ops:
  0.6 65.8 %elastic_up_backward.1 = (bf16[256,384]{1,0:T(8,128)(2,1)}, bf16[192,1536]{1,0:T(8,128)(2,1)}) custom-call(bf16[256,384]{1,0:T(8,128)(2,1)} %x_ref.1, bf16[256,1536]{1,0:T(8,128)(2,1)} %g_ref.1, bf16[192,1536]{1,0:T(8,128)(2,1)} %w_ref.1, s32[2,128]{1,0:T(2,128)} %bitcast.1), custom_call_target="tpu_custom_call" | custom-call | flops 7247757312 | bytes 4194304 | tf_op jit(solution)/shard_map/elastic_up_backward/pallas_call | solution.py:569
  66.5 1.9 %hand_on.1 = (bf16[256,384]{1,0:T(8,128)(2,1)}, bf16[192,1536]{1,0:T(8,128)(2,1)}) custom-call(bf16[256,384]{1,0:T(8,128)(2,1)} %get-tuple-element.4.a_ref, bf16[192,1536]{1,0:T(8,128)(2,1)} %get-tuple-element.5.b_ref), custom_call_target="tpu_custom_call" | custom-call | tf_op jit(solution)/shard_map/hand_on/pallas_call | solution.py:612

commit v9 on v7

--- a/solution.py
+++ b/solution.py
@@ -28,8 +28,8 @@
     "zfp1", "xy3", "zdm2", "zfm1", "zfp3", "zfm3", "zl2", "zdp1", "zdm1", "zdm3", "yfm3", "zdp3", "g2",
     "yfp3", "wr1", "zl1", "Pa0", "zl3", "PaA", "wr2", "PbA", "IA1", "IA3", "Pb0", "Pb3", "D20", "IB2",
     "IA2", "IA0", "D21", "E20", "D10", "IB3", "IB1", "D30", "E21", "D31", "D11", "E10", "R1", "E30", "D00",
-    "D01", "E31", "E11", "Zc1", "R2", "Zd0", "Zc0", "Zc2", "E00", "Zd1", "Zd2", "Zd3", "IB0", "sent", "E01",
-    "S0", "Zc3", "R3", "ZL0", "Vp", "Vm", "ZL1", "ZL2", "R0", "ZL3", "RF",
+    "D01", "E31", "E11", "Zc1", "R2", "Zd0", "Zc0", "Zc2", "E00", "Zd1", "Zd2", "Zd3", "IB0", "E01",
+    "S0", "Zc3", "R3", "sent", "ZL0", "Vp", "Vm", "ZL1", "ZL2", "R0", "ZL3", "RF",
 )
 
 def kernel(

time: 68.2 us -> 68.2 us (level)
  no operation moved by 1% of the time
where the time goes in v9:
time: 68.2 us; the launch traced here: 68 us
  Pallas kernels  67.4 us (99%)
    pallas_call x1, Pallas kernels, shards(): pl.pallas_call(kernel, out_shape=results, in_specs=[any_space] * 4, out_s...  65.5 us
    pallas_call x1, Pallas kernels, shards(): pl.pallas_call(hand_on, out_shape=results, in_specs=[any_space] * 2, out_...  1.89 us

profile of v9, /device:TPU:1, one launch (start us, length us, event | category | flops | bytes accessed | tf_op | source)
XLA Modules:
  0.0 68.0 jit_solution(10065893008635523511)
XLA Ops:
  0.6 65.5 %elastic_up_backward.1 = (bf16[256,384]{1,0:T(8,128)(2,1)}, bf16[192,1536]{1,0:T(8,128)(2,1)}) custom-call(bf16[256,384]{1,0:T(8,128)(2,1)} %x_ref.1, bf16[256,1536]{1,0:T(8,128)(2,1)} %g_ref.1, bf16[192,1536]{1,0:T(8,128)(2,1)} %w_ref.1, s32[2,128]{1,0:T(2,128)} %bitcast.1), custom_call_target="tpu_custom_call" | custom-call | flops 7247757312 | bytes 4194304 | tf_op jit(solution)/shard_map/elastic_up_backward/pallas_call | solution.py:569
  66.1 1.9 %hand_on.1 = (bf16[256,384]{1,0:T(8,128)(2,1)}, bf16[192,1536]{1,0:T(8,128)(2,1)}) custom-call(bf16[256,384]{1,0:T(8,128)(2,1)} %get-tuple-element.4.a_ref, bf16[192,1536]{1,0:T(8,128)(2,1)} %get-tuple-element.5.b_ref), custom_call_target="tpu_custom_call" | custom-call | tf_op jit(solution)/shard_map/hand_on/pallas_call | solution.py:612
